TPU v7x, 128 devices: a whole 4x4x4 slice. The times are simulated.
128 devices in a mesh: ctx: 16 (over x, y), head: 8 (over z, core).
Axes of the slice: x: 4, y: 4, z: 4, core: 2. Of those that a mesh axis runs over, the one named last changes fastest.
Arguments:
- query: bfloat16 [16384, 3072], P('ctx', 'head'), may hold values from -110 to 110
- keys: bfloat16 [16384, 3072], P('ctx', 'head'), may hold values from -5 to 5
- values: bfloat16 [16384, 3072], P('ctx', 'head'), may hold values from -6 to 6
- doc_lengths: int32 [8], replicated, may hold values from 1 to 8192, as said below
- w_out: bfloat16 [3072, 5120], P('head'), may hold values from -0.15625 to 0.15625
Outputs:
- layer_out: bfloat16 [16384, 5120], P('ctx', 'head')
Inputs may be any that keep to these rules, and one draw needn't show every extreme that they name: `doc_lengths`: 8 document lengths summing to 16384; the first document has exactly 8192 tokens and every other one fewer.
All inputs are finite; a program needn't handle non-finite values.
Results may differ from a plain program's by a relative error of at most 0.018.
Values may be sent and summed in bfloat16 or wider, within the bound.
A program may use at most 128 MiB of HBM per device.

v0:
```python
import math

import jax
import jax.numpy as jnp
from jax import lax
from jax.sharding import PartitionSpec as P

HD = 128


def passed_along(value, axis, by):
    size = lax.axis_size(axis)
    pairs = [(i, i + by) for i in range(size) if 0 <= i + by < size]
    return lax.ppermute(value, axis, pairs)


def doc_of(places, ends):
    return jnp.sum((places[:, None] >= ends[None, :]).astype(jnp.int32), axis=1)


def update(state, query_part, query_pos, query_doc, key_part, value_part, key_pos, key_doc, scale):
    top, total, accum = state
    scores = (
        jnp.einsum("qhd,khd->hqk", query_part, key_part, preferred_element_type=jnp.float32) * scale
    )
    allowed = (key_pos[None, :] <= query_pos[:, None]) & (key_doc[None, :] == query_doc[:, None])
    scores = jnp.where(allowed[None], scores, -1e30)
    new_top = jnp.maximum(top, jnp.max(scores, axis=2))
    weights = jnp.where(allowed[None], jnp.exp(scores - new_top[:, :, None]), 0.0)
    shrink = jnp.exp(top - new_top)
    total = total * shrink + jnp.sum(weights, axis=2)
    mixed = jnp.einsum(
        "hqk,khd->hqd", weights.astype(jnp.bfloat16), value_part, preferred_element_type=jnp.float32
    )
    accum = accum * shrink[:, :, None] + mixed
    return (new_top, total, accum)


def visit(state, query_part, query_pos, query_doc, key_part, value_part, key_pos, key_doc, scale):
    masked = (key_pos[0] > query_pos[-1]) | (key_doc[-1] < query_doc[0])
    return lax.cond(
        masked,
        lambda current: current,
        lambda current: update(
            current, query_part, query_pos, query_doc, key_part, value_part, key_pos, key_doc, scale
        ),
        state,
    )


def per_device(query, keys, values, doc_lengths, w_out):
    rows, width = query.shape
    heads = width // HD
    count = lax.axis_size("ctx")
    device = lax.axis_index("ctx")
    ends = jnp.cumsum(doc_lengths)
    scale = 1.0 / math.sqrt(HD)
    query_parts = [query]
    kv_local = jnp.stack([keys, values])

    def starts(owner):
        return [owner * rows]

    parts = len(query_parts)
    kv_local = kv_local.reshape(2 * parts, rows, heads, HD)
    query_three = [part_rows.reshape(rows, heads, HD) for part_rows in query_parts]
    offsets = jnp.arange(rows, dtype=jnp.int32)
    query_pos = [first + offsets for first in starts(device)]
    query_doc = [doc_of(places, ends) for places in query_pos]

    def visit_all(states, kv_now, source):
        key_pos = [first + offsets for first in starts(source)]
        key_doc = [doc_of(places, ends) for places in key_pos]
        current = states[0]
        current = visit(
            current,
            query_three[0],
            query_pos[0],
            query_doc[0],
            kv_now[0],
            kv_now[parts],
            key_pos[0],
            key_doc[0],
            scale,
        )
        updated = [current]
        return tuple(updated)

    blank = (
        jnp.full((heads, rows), -1e30, jnp.float32),
        jnp.zeros((heads, rows), jnp.float32),
        jnp.zeros((heads, rows, HD), jnp.float32),
    )
    states = tuple((blank for left in range(parts)))

    def pass_far(step, carry):
        kv_now, current = carry
        current = visit_all(current, kv_now, (device - step) % count)
        kv_now = passed_along(kv_now, "ctx", 1)
        return (kv_now, current)

    reach = count - 1
    kv_now, states = lax.fori_loop(0, reach, pass_far, (kv_local, states))
    states = visit_all(states, kv_now, (device - reach) % count)
    results = [
        (accum / total[:, :, None]).transpose(1, 0, 2).reshape(rows, width).astype(jnp.bfloat16)
        for top, total, accum in states
    ]
    attended = results[0]
    projected = jnp.dot(attended, w_out, preferred_element_type=jnp.float32)
    return lax.psum_scatter(projected.astype(jnp.bfloat16), "head", scatter_dimension=1, tiled=True)


def solution(mesh):
    return jax.shard_map(
        per_device,
        mesh=mesh,
        in_specs=(P("ctx", "head"), P("ctx", "head"), P("ctx", "head"), P(), P("head", None)),
        out_specs=P("ctx", "head"),
        check_vma=False,
    )
```

profile of v0, /device:TPU:1, one launch (start us, length us, event | category | flops | bytes accessed | tf_op | source)
XLA Modules:
  0.0 659.0 jit_solution(7393186702938257996)
XLA Ops:
  18.9 518.0 %while.22 = (s32[]{:T(128)}, bf16[2,1024,3,128]{3,1,2,0:T(8,128)(2,1)S(1)}, f32[3,1024]{1,0:T(4,128)S(1)}, f32[3,1024]{1,0:T(4,128)S(1)}, f32[3,1024,128]{2,1,0:...) while((s32[]{:T(128)}, ...), condition=%wide.region_9.10_spmd.clone, body=%wide.region_3.9_spmd.clone.sunk | while | flops 1655470080 | bytes 57111056 | solution.py:103
  29.0 15.3 %conditional.5 = (f32[3,1024]{1,0:T(4,128)S(1)}, f32[3,1024]{1,0:T(4,128)S(1)}, f32[3,1024,128]{2,1,0:T(8,128)S(1)}) conditional(s32[]{:T(128)} %bitcast.33, (s32[1024]{0:T(1024)S(1)}, s32[1024]{0:T(1024)S(1)}, s32[1024]{0:T(1024)S(1)}, s32[1024]{0:T(1024)S(1)}, bf16[2,1024,3,128]{3,1,2,0:T(8,128)(2,1)}, /*index=5*/bf16[1024,3,128]{2,0,1:T(8,128)(2,1)}, ...), branch_computations={%region_5.7_spmd, %region_8.8_spmd} | conditional | flops 1655445504 | bytes 47636504 | solution.py:41
  37.6 6.7 %multiply_add_fusion = f32[3,1024,128]{2,1,0:T(8,128)S(1)} fusion(f32[3,1024,128]{2,1,0:T(8,128)S(1)} %get-tuple-element.336, f32[3,1024,1024]{1,2,0:T(8,128)S(1)} %get-tuple-element.485, f32[3,1024]{1,0:T(4,128)S(1)} %max.4, pred[1024,1024]{0,1:T(8,128)(4,1)S(1)} %compare_and_fusion, bf16[2,1024,3,128]{3,1,2,0:T(8,128)(2,1)} %get-tuple-element.334, ...), kind=kOutput, calls=%fused_computation.9 | convolution fusion | flops 821821440 | bytes 17588224 | tf_op jit(solution)/shard_map/while/body/eval_jaxpr/cond/branch_0_fun/hqk,khd->hqd/dot_general | solution.py:32
  44.3 13.1 %collective-permute-done = bf16[2,1024,3,128]{3,1,2,0:T(8,128)(2,1)S(1)} collective-permute-done((bf16[2,1024,3,128]{3,1,2,0:T(8,128)(2,1)}, bf16[2,1024,3,128]{3,1,2,0:T(8,128)(2,1)S(1)}, u32[]{:S(2)}, u32[]{:S(2)}) %collective-permute-start) | collective-permute-done | bytes 1572896 | tf_op jit(solution)/shard_map/while/body/eval_jaxpr/ppermute | solution.py:14
  67.6 27.4 %collective-permute-done = bf16[2,1024,3,128]{3,1,2,0:T(8,128)(2,1)S(1)} collective-permute-done((bf16[2,1024,3,128]{3,1,2,0:T(8,128)(2,1)}, bf16[2,1024,3,128]{3,1,2,0:T(8,128)(2,1)S(1)}, u32[]{:S(2)}, u32[]{:S(2)}) %collective-permute-start) | collective-permute-done | bytes 1572896 | tf_op jit(solution)/shard_map/while/body/eval_jaxpr/ppermute | solution.py:14
  105.2 26.5 %collective-permute-done = bf16[2,1024,3,128]{3,1,2,0:T(8,128)(2,1)S(1)} collective-permute-done((bf16[2,1024,3,128]{3,1,2,0:T(8,128)(2,1)}, bf16[2,1024,3,128]{3,1,2,0:T(8,128)(2,1)S(1)}, u32[]{:S(2)}, u32[]{:S(2)}) %collective-permute-start) | collective-permute-done | bytes 1572896 | tf_op jit(solution)/shard_map/while/body/eval_jaxpr/ppermute | solution.py:14
  141.8 25.6 %collective-permute-done = bf16[2,1024,3,128]{3,1,2,0:T(8,128)(2,1)S(1)} collective-permute-done((bf16[2,1024,3,128]{3,1,2,0:T(8,128)(2,1)}, bf16[2,1024,3,128]{3,1,2,0:T(8,128)(2,1)S(1)}, u32[]{:S(2)}, u32[]{:S(2)}) %collective-permute-start) | collective-permute-done | bytes 1572896 | tf_op jit(solution)/shard_map/while/body/eval_jaxpr/ppermute | solution.py:14
  177.6 24.7 %collective-permute-done = bf16[2,1024,3,128]{3,1,2,0:T(8,128)(2,1)S(1)} collective-permute-done((bf16[2,1024,3,128]{3,1,2,0:T(8,128)(2,1)}, bf16[2,1024,3,128]{3,1,2,0:T(8,128)(2,1)S(1)}, u32[]{:S(2)}, u32[]{:S(2)}) %collective-permute-start) | collective-permute-done | bytes 1572896 | tf_op jit(solution)/shard_map/while/body/eval_jaxpr/ppermute | solution.py:14
  213.5 23.8 %collective-permute-done = bf16[2,1024,3,128]{3,1,2,0:T(8,128)(2,1)S(1)} collective-permute-done((bf16[2,1024,3,128]{3,1,2,0:T(8,128)(2,1)}, bf16[2,1024,3,128]{3,1,2,0:T(8,128)(2,1)S(1)}, u32[]{:S(2)}, u32[]{:S(2)}) %collective-permute-start) | collective-permute-done | bytes 1572896 | tf_op jit(solution)/shard_map/while/body/eval_jaxpr/ppermute | solution.py:14
  238.4 6.2 collective-permute-start
  249.5 22.8 %collective-permute-done = bf16[2,1024,3,128]{3,1,2,0:T(8,128)(2,1)S(1)} collective-permute-done((bf16[2,1024,3,128]{3,1,2,0:T(8,128)(2,1)}, bf16[2,1024,3,128]{3,1,2,0:T(8,128)(2,1)S(1)}, u32[]{:S(2)}, u32[]{:S(2)}) %collective-permute-start) | collective-permute-done | bytes 1572896 | tf_op jit(solution)/shard_map/while/body/eval_jaxpr/ppermute | solution.py:14
  284.6 21.9 %collective-permute-done = bf16[2,1024,3,128]{3,1,2,0:T(8,128)(2,1)S(1)} collective-permute-done((bf16[2,1024,3,128]{3,1,2,0:T(8,128)(2,1)}, bf16[2,1024,3,128]{3,1,2,0:T(8,128)(2,1)S(1)}, u32[]{:S(2)}, u32[]{:S(2)}) %collective-permute-start) | collective-permute-done | bytes 1572896 | tf_op jit(solution)/shard_map/while/body/eval_jaxpr/ppermute | solution.py:14
  318.8 21.0 %collective-permute-done = bf16[2,1024,3,128]{3,1,2,0:T(8,128)(2,1)S(1)} collective-permute-done((bf16[2,1024,3,128]{3,1,2,0:T(8,128)(2,1)}, bf16[2,1024,3,128]{3,1,2,0:T(8,128)(2,1)S(1)}, u32[]{:S(2)}, u32[]{:S(2)}) %collective-permute-start) | collective-permute-done | bytes 1572896 | tf_op jit(solution)/shard_map/while/body/eval_jaxpr/ppermute | solution.py:14
  340.9 6.2 collective-permute-start
  352.0 20.6 %collective-permute-done = bf16[2,1024,3,128]{3,1,2,0:T(8,128)(2,1)S(1)} collective-permute-done((bf16[2,1024,3,128]{3,1,2,0:T(8,128)(2,1)}, bf16[2,1024,3,128]{3,1,2,0:T(8,128)(2,1)S(1)}, u32[]{:S(2)}, u32[]{:S(2)}) %collective-permute-start) | collective-permute-done | bytes 1572896 | tf_op jit(solution)/shard_map/while/body/eval_jaxpr/ppermute | solution.py:14
  373.8 6.2 collective-permute-start
  384.9 20.6 %collective-permute-done = bf16[2,1024,3,128]{3,1,2,0:T(8,128)(2,1)S(1)} collective-permute-done((bf16[2,1024,3,128]{3,1,2,0:T(8,128)(2,1)}, bf16[2,1024,3,128]{3,1,2,0:T(8,128)(2,1)S(1)}, u32[]{:S(2)}, u32[]{:S(2)}) %collective-permute-start) | collective-permute-done | bytes 1572896 | tf_op jit(solution)/shard_map/while/body/eval_jaxpr/ppermute | solution.py:14
  417.7 20.6 %collective-permute-done = bf16[2,1024,3,128]{3,1,2,0:T(8,128)(2,1)S(1)} collective-permute-done((bf16[2,1024,3,128]{3,1,2,0:T(8,128)(2,1)}, bf16[2,1024,3,128]{3,1,2,0:T(8,128)(2,1)S(1)}, u32[]{:S(2)}, u32[]{:S(2)}) %collective-permute-start) | collective-permute-done | bytes 1572896 | tf_op jit(solution)/shard_map/while/body/eval_jaxpr/ppermute | solution.py:14
  450.6 20.6 %collective-permute-done = bf16[2,1024,3,128]{3,1,2,0:T(8,128)(2,1)S(1)} collective-permute-done((bf16[2,1024,3,128]{3,1,2,0:T(8,128)(2,1)}, bf16[2,1024,3,128]{3,1,2,0:T(8,128)(2,1)S(1)}, u32[]{:S(2)}, u32[]{:S(2)}) %collective-permute-start) | collective-permute-done | bytes 1572896 | tf_op jit(solution)/shard_map/while/body/eval_jaxpr/ppermute | solution.py:14
  483.4 20.6 %collective-permute-done = bf16[2,1024,3,128]{3,1,2,0:T(8,128)(2,1)S(1)} collective-permute-done((bf16[2,1024,3,128]{3,1,2,0:T(8,128)(2,1)}, bf16[2,1024,3,128]{3,1,2,0:T(8,128)(2,1)S(1)}, u32[]{:S(2)}, u32[]{:S(2)}) %collective-permute-start) | collective-permute-done | bytes 1572896 | tf_op jit(solution)/shard_map/while/body/eval_jaxpr/ppermute | solution.py:14
  516.3 20.6 %collective-permute-done = bf16[2,1024,3,128]{3,1,2,0:T(8,128)(2,1)S(1)} collective-permute-done((bf16[2,1024,3,128]{3,1,2,0:T(8,128)(2,1)}, bf16[2,1024,3,128]{3,1,2,0:T(8,128)(2,1)S(1)}, u32[]{:S(2)}, u32[]{:S(2)}) %collective-permute-start) | collective-permute-done | bytes 1572896 | tf_op jit(solution)/shard_map/while/body/eval_jaxpr/ppermute | solution.py:14
  537.5 10.2 %convolution_convert_fusion = bf16[1024,5120]{1,0:T(8,128)(2,1)} fusion(bf16[1024,384]{0,1:T(8,128)(2,1)S(1)} %bitcast.40, bf16[384,5120]{1,0:T(8,128)(2,1)} %param.15), kind=kOutput, calls=%fused_computation.41 | convolution fusion | flops 4031774720 | bytes 15204352 | tf_op jit(solution)/shard_map/dot_general | solution.py:110
  547.8 14.4 %copy.38 = bf16[1024,5120]{0,1:T(8,128)(2,1)} copy(bf16[1024,5120]{1,0:T(8,128)(2,1)} %convolution_convert_fusion) | data formatting | bytes 20971520
  562.2 87.5 %reduce-scatter.4.cloned.1.call-done = bf16[640,1024]{1,0:T(8,128)(2,1)} async-done(((bf16[5120,1024]{1,0:T(8,128)(2,1)}), bf16[640,1024]{1,0:T(8,128)(2,1)}) %reduce-scatter.4.cloned.1.call-update) | async-done | bytes 1310736
  (189 shorter events, 138.4 us)
Async XLA Ops:
  6.5 643.2 %reduce-scatter.4.cloned.1.call-start = ((), (), s32[]{:S(2)}) async-start(), calls=%async_computation.1 | async-start | bytes 11796480
  13.7 4.0 copy-start
  20.0 37.4 %collective-permute-start = (bf16[2,1024,3,128]{3,1,2,0:T(8,128)(2,1)}, bf16[2,1024,3,128]{3,1,2,0:T(8,128)(2,1)S(1)}, u32[]{:S(2)}, u32[]{:S(2)}) collective-permute-start(bf16[2,1024,3,128]{3,1,2,0:T(8,128)(2,1)} %copy.54), channel_id=1, source_target_pairs={{0,8},{8,16},{16,24},{24,32},{32,40},{40,48},{48,56},{56,64},{64,7... | collective-permute-start | bytes 4718600 | tf_op jit(solution)/shard_map/while/body/eval_jaxpr/ppermute | solution.py:14
  58.6 36.4 %collective-permute-start = (bf16[2,1024,3,128]{3,1,2,0:T(8,128)(2,1)}, bf16[2,1024,3,128]{3,1,2,0:T(8,128)(2,1)S(1)}, u32[]{:S(2)}, u32[]{:S(2)}) collective-permute-start(bf16[2,1024,3,128]{3,1,2,0:T(8,128)(2,1)} %copy.54), channel_id=1, source_target_pairs={{0,8},{8,16},{16,24},{24,32},{32,40},{40,48},{48,56},{56,64},{64,7... | collective-permute-start | bytes 4718600 | tf_op jit(solution)/shard_map/while/body/eval_jaxpr/ppermute | solution.py:14
  96.2 35.5 %collective-permute-start = (bf16[2,1024,3,128]{3,1,2,0:T(8,128)(2,1)}, bf16[2,1024,3,128]{3,1,2,0:T(8,128)(2,1)S(1)}, u32[]{:S(2)}, u32[]{:S(2)}) collective-permute-start(bf16[2,1024,3,128]{3,1,2,0:T(8,128)(2,1)} %copy.54), channel_id=1, source_target_pairs={{0,8},{8,16},{16,24},{24,32},{32,40},{40,48},{48,56},{56,64},{64,7... | collective-permute-start | bytes 4718600 | tf_op jit(solution)/shard_map/while/body/eval_jaxpr/ppermute | solution.py:14
  132.8 34.6 %collective-permute-start = (bf16[2,1024,3,128]{3,1,2,0:T(8,128)(2,1)}, bf16[2,1024,3,128]{3,1,2,0:T(8,128)(2,1)S(1)}, u32[]{:S(2)}, u32[]{:S(2)}) collective-permute-start(bf16[2,1024,3,128]{3,1,2,0:T(8,128)(2,1)} %copy.54), channel_id=1, source_target_pairs={{0,8},{8,16},{16,24},{24,32},{32,40},{40,48},{48,56},{56,64},{64,7... | collective-permute-start | bytes 4718600 | tf_op jit(solution)/shard_map/while/body/eval_jaxpr/ppermute | solution.py:14
  168.6 33.7 %collective-permute-start = (bf16[2,1024,3,128]{3,1,2,0:T(8,128)(2,1)}, bf16[2,1024,3,128]{3,1,2,0:T(8,128)(2,1)S(1)}, u32[]{:S(2)}, u32[]{:S(2)}) collective-permute-start(bf16[2,1024,3,128]{3,1,2,0:T(8,128)(2,1)} %copy.54), channel_id=1, source_target_pairs={{0,8},{8,16},{16,24},{24,32},{32,40},{40,48},{48,56},{56,64},{64,7... | collective-permute-start | bytes 4718600 | tf_op jit(solution)/shard_map/while/body/eval_jaxpr/ppermute | solution.py:14
  203.4 33.8 %collective-permute-start = (bf16[2,1024,3,128]{3,1,2,0:T(8,128)(2,1)}, bf16[2,1024,3,128]{3,1,2,0:T(8,128)(2,1)S(1)}, u32[]{:S(2)}, u32[]{:S(2)}) collective-permute-start(bf16[2,1024,3,128]{3,1,2,0:T(8,128)(2,1)} %copy.54), channel_id=1, source_target_pairs={{0,8},{8,16},{16,24},{24,32},{32,40},{40,48},{48,56},{56,64},{64,7... | collective-permute-start | bytes 4718600 | tf_op jit(solution)/shard_map/while/body/eval_jaxpr/ppermute | solution.py:14
  238.4 33.9 %collective-permute-start = (bf16[2,1024,3,128]{3,1,2,0:T(8,128)(2,1)}, bf16[2,1024,3,128]{3,1,2,0:T(8,128)(2,1)S(1)}, u32[]{:S(2)}, u32[]{:S(2)}) collective-permute-start(bf16[2,1024,3,128]{3,1,2,0:T(8,128)(2,1)} %copy.54), channel_id=1, source_target_pairs={{0,8},{8,16},{16,24},{24,32},{32,40},{40,48},{48,56},{56,64},{64,7... | collective-permute-start | bytes 4718600 | tf_op jit(solution)/shard_map/while/body/eval_jaxpr/ppermute | solution.py:14
  273.5 33.0 %collective-permute-start = (bf16[2,1024,3,128]{3,1,2,0:T(8,128)(2,1)}, bf16[2,1024,3,128]{3,1,2,0:T(8,128)(2,1)S(1)}, u32[]{:S(2)}, u32[]{:S(2)}) collective-permute-start(bf16[2,1024,3,128]{3,1,2,0:T(8,128)(2,1)} %copy.54), channel_id=1, source_target_pairs={{0,8},{8,16},{16,24},{24,32},{32,40},{40,48},{48,56},{56,64},{64,7... | collective-permute-start | bytes 4718600 | tf_op jit(solution)/shard_map/while/body/eval_jaxpr/ppermute | solution.py:14
  307.7 32.1 %collective-permute-start = (bf16[2,1024,3,128]{3,1,2,0:T(8,128)(2,1)}, bf16[2,1024,3,128]{3,1,2,0:T(8,128)(2,1)S(1)}, u32[]{:S(2)}, u32[]{:S(2)}) collective-permute-start(bf16[2,1024,3,128]{3,1,2,0:T(8,128)(2,1)} %copy.54), channel_id=1, source_target_pairs={{0,8},{8,16},{16,24},{24,32},{32,40},{40,48},{48,56},{56,64},{64,7... | collective-permute-start | bytes 4718600 | tf_op jit(solution)/shard_map/while/body/eval_jaxpr/ppermute | solution.py:14
  340.9 31.7 %collective-permute-start = (bf16[2,1024,3,128]{3,1,2,0:T(8,128)(2,1)}, bf16[2,1024,3,128]{3,1,2,0:T(8,128)(2,1)S(1)}, u32[]{:S(2)}, u32[]{:S(2)}) collective-permute-start(bf16[2,1024,3,128]{3,1,2,0:T(8,128)(2,1)} %copy.54), channel_id=1, source_target_pairs={{0,8},{8,16},{16,24},{24,32},{32,40},{40,48},{48,56},{56,64},{64,7... | collective-permute-start | bytes 4718600 | tf_op jit(solution)/shard_map/while/body/eval_jaxpr/ppermute | solution.py:14
  373.8 31.7 %collective-permute-start = (bf16[2,1024,3,128]{3,1,2,0:T(8,128)(2,1)}, bf16[2,1024,3,128]{3,1,2,0:T(8,128)(2,1)S(1)}, u32[]{:S(2)}, u32[]{:S(2)}) collective-permute-start(bf16[2,1024,3,128]{3,1,2,0:T(8,128)(2,1)} %copy.54), channel_id=1, source_target_pairs={{0,8},{8,16},{16,24},{24,32},{32,40},{40,48},{48,56},{56,64},{64,7... | collective-permute-start | bytes 4718600 | tf_op jit(solution)/shard_map/while/body/eval_jaxpr/ppermute | solution.py:14
  406.6 31.7 %collective-permute-start = (bf16[2,1024,3,128]{3,1,2,0:T(8,128)(2,1)}, bf16[2,1024,3,128]{3,1,2,0:T(8,128)(2,1)S(1)}, u32[]{:S(2)}, u32[]{:S(2)}) collective-permute-start(bf16[2,1024,3,128]{3,1,2,0:T(8,128)(2,1)} %copy.54), channel_id=1, source_target_pairs={{0,8},{8,16},{16,24},{24,32},{32,40},{40,48},{48,56},{56,64},{64,7... | collective-permute-start | bytes 4718600 | tf_op jit(solution)/shard_map/while/body/eval_jaxpr/ppermute | solution.py:14
  439.5 31.7 %collective-permute-start = (bf16[2,1024,3,128]{3,1,2,0:T(8,128)(2,1)}, bf16[2,1024,3,128]{3,1,2,0:T(8,128)(2,1)S(1)}, u32[]{:S(2)}, u32[]{:S(2)}) collective-permute-start(bf16[2,1024,3,128]{3,1,2,0:T(8,128)(2,1)} %copy.54), channel_id=1, source_target_pairs={{0,8},{8,16},{16,24},{24,32},{32,40},{40,48},{48,56},{56,64},{64,7... | collective-permute-start | bytes 4718600 | tf_op jit(solution)/shard_map/while/body/eval_jaxpr/ppermute | solution.py:14
  472.3 31.7 %collective-permute-start = (bf16[2,1024,3,128]{3,1,2,0:T(8,128)(2,1)}, bf16[2,1024,3,128]{3,1,2,0:T(8,128)(2,1)S(1)}, u32[]{:S(2)}, u32[]{:S(2)}) collective-permute-start(bf16[2,1024,3,128]{3,1,2,0:T(8,128)(2,1)} %copy.54), channel_id=1, source_target_pairs={{0,8},{8,16},{16,24},{24,32},{32,40},{40,48},{48,56},{56,64},{64,7... | collective-permute-start | bytes 4718600 | tf_op jit(solution)/shard_map/while/body/eval_jaxpr/ppermute | solution.py:14
  505.2 31.7 %collective-permute-start = (bf16[2,1024,3,128]{3,1,2,0:T(8,128)(2,1)}, bf16[2,1024,3,128]{3,1,2,0:T(8,128)(2,1)S(1)}, u32[]{:S(2)}, u32[]{:S(2)}) collective-permute-start(bf16[2,1024,3,128]{3,1,2,0:T(8,128)(2,1)} %copy.54), channel_id=1, source_target_pairs={{0,8},{8,16},{16,24},{24,32},{32,40},{40,48},{48,56},{56,64},{64,7... | collective-permute-start | bytes 4718600 | tf_op jit(solution)/shard_map/while/body/eval_jaxpr/ppermute | solution.py:14
Sparse Core Ops, SparseCore 0:
  562.3 87.3 reduce-scatter.3
where the time goes:
time: 661 us; the launch traced here: 659 us
  waiting for transfers between devices  418 us (63%)
  starting transfers between devices  81.4 us (12%)
  local copies, waits for them, and re-layouts  78 us (12%)
  loops' own time  37.6 us (6%)
  matrix products  20.9 us (3%)
  between operations  16 us (2%)
  other arithmetic  7.05 us (1%)
    ppermute x15, waiting for transfers between devices, passed_along(): return lax.ppermute(value, axis, pairs)  330 us
    unnamed x2, waiting for transfers between devices  87.6 us
    ppermute x15, starting transfers between devices, passed_along(): return lax.ppermute(value, axis, pairs)  81.4 us
    another operation x1, loops' own time, per_device(): kv_now, states = lax.fori_loop(0, reach, pass_far, (kv_local, states))  37.1 us
    slice x64, local copies, waits for them, and re-layouts, visit(): masked = (key_pos[0] > query_pos[-1]) | (key_doc[-1] < query_doc[0])  36.9 us
    unnamed x9, local copies, waits for them, and re-layouts  23.1 us
    while x30, local copies, waits for them, and re-layouts  17.4 us
  transfers between devices with their start and end apart: 16, of which 16 were waited for; matrix products, arithmetic and copies ran while one was open for 8% of the time, Pallas kernels for 0%

commit v1 on v0

v1 whole, which is shorter than its diff:
```python
import functools
import math

import jax
import jax.numpy as jnp
from jax import lax
from jax.experimental import pallas as pl
from jax.experimental.pallas import tpu as pltpu
from jax.sharding import PartitionSpec as P

HD = 128
BLOCKS = 8
RING = 4
MASKED = -1e30
FLOOR = -1e29
MESH = pl.DeviceIdType.MESH


def kernel(
    lengths_ref, q_ref, k_ref, v_ref, w_ref, out_ref,
    q_in, kv_in, q_two, keys_across, low, top, accum, scores, shares, mixed, gathered, weights, total,
    send_sem, q_sem, kv_sem, share_send, share_sem, mixed_send, mixed_sem,
    w_send, w_sem, across_send, across_sem, ring_send, ring_sem, relay_send, relay_sem, pair_send, pair_sem,
):
    rows = q_ref.shape[0]
    part = rows // 2
    heads = q_ref.shape[1] // HD
    width = heads * HD
    out_cols = out_ref.shape[1]
    ctx, head = lax.axis_index("ctx"), lax.axis_index("head")
    half, place = ctx // BLOCKS, lax.rem(ctx, BLOCKS)
    place_x, place_y = place // RING, lax.rem(place, RING)
    z, core = head // 2, lax.rem(head, 2)
    other = 1 - core
    first = half * BLOCKS
    sibling = (ctx, z * 2 + other)
    z_up, z_down, z_far = lax.rem(z + 1, RING), lax.rem(z + 3, RING), lax.rem(z + 2, RING)
    works = place_y < heads
    partner = ((RING - 1 - ctx // RING) * RING + place_y, head)

    barrier = pltpu.get_barrier_semaphore()
    for block in range(BLOCKS):
        for c in range(2):
            @pl.when((block != place) | (c != core))
            def _():
                pl.semaphore_signal(
                    barrier, inc=1, device_id=(first + block, z * 2 + c), device_id_type=MESH
                )
    for away in range(1, RING):
        for c in range(2):
            pl.semaphore_signal(
                barrier, inc=1, device_id=(ctx, lax.rem(z + away, RING) * 2 + c), device_id_type=MESH
            )
    pl.semaphore_signal(barrier, inc=1, device_id=partner, device_id_type=MESH)
    pl.semaphore_wait(barrier, 2 * BLOCKS - 1 + 2 * (RING - 1) + 1)

    def outgoing(away, c, n):
        local = lax.rem(place_y + away, RING)
        target = core * RING + local
        cols = pl.ds(pl.multiple_of(local * HD, HD), HD)
        span = pl.ds(c * part, part)
        source, dest, sem = (
            (k_ref, kv_in.at[place, 0, span], kv_sem.at[place]),
            (v_ref, kv_in.at[place, 1, span], kv_sem.at[place]),
            (q_ref, q_in.at[place], q_sem.at[place]),
        )[n]
        here = target == place

        def remote():
            return pltpu.make_async_remote_copy(
                src_ref=source.at[span, cols], dst_ref=dest, send_sem=send_sem.at[away, c, n], recv_sem=sem,
                device_id=(first + target, z * 2 + c), device_id_type=MESH,
            )

        def start():
            if away == 0:
                @pl.when((local < heads) & here & (core == c))
                def _():
                    pltpu.make_async_copy(source.at[span, cols], dest, sem).start()

                @pl.when((local < heads) & jnp.logical_not(here & (core == c)))
                def _():
                    remote().start()
            else:
                @pl.when(local < heads)
                def _():
                    remote().start()

        def finish():
            sent = local < heads
            if away == 0:
                sent &= jnp.logical_not(here & (core == c))

            @pl.when(sent)
            def _():
                remote().wait_send()

        return start, finish

    def weight_cols(target):
        return pl.ds(pl.multiple_of(target * out_cols, 128), out_cols)

    def weight_copy(away, c):
        target = lax.rem(z + away, RING) * 2 + c
        return pltpu.make_async_remote_copy(
            src_ref=w_ref.at[half, :, weight_cols(target)], dst_ref=weights.at[z, core, half],
            send_sem=w_send.at[away, c], recv_sem=w_sem.at[z, core],
            device_id=(ctx, target), device_id_type=MESH,
        )

    def weight_pair():
        return pltpu.make_async_remote_copy(
            src_ref=w_ref.at[:, :, weight_cols(z * 2 + other)], dst_ref=weights.at[z, core],
            send_sem=w_send.at[0, 0], recv_sem=w_sem.at[z, core],
            device_id=sibling, device_id_type=MESH,
        )

    def weight_across(away):
        piece = weights.at[lax.rem(z + away, RING), :, half]
        return pltpu.make_async_remote_copy(
            src_ref=piece, dst_ref=piece, send_sem=across_send.at[away], recv_sem=across_sem.at[away],
            device_id=partner, device_id_type=MESH,
        )

    def hand_across(away):
        source = lax.rem(z + away, RING)
        for c in range(2):
            piece = weights.at[source, c, half]
            pltpu.make_async_copy(piece, piece, w_sem.at[source, c]).wait()
        weight_across(away).start()

    def weights_here(away):
        source = lax.rem(z + away, RING)
        if away == 0:
            for c in range(2):
                piece = weights.at[source, c]
                pltpu.make_async_copy(piece, piece, w_sem.at[source, c]).wait()
        else:
            piece = weights.at[source, :, 1 - half]
            pltpu.make_async_copy(piece, piece, across_sem.at[away]).wait()

    sends = [[outgoing(away, c, n) for away in (1, 3, 2, 0) for c in range(2)] for n in range(3)]
    for group, away in zip(sends, (2, 1, 3)):
        for start, _ in group:
            start()
        for c in range(2):
            weight_copy(away, c).start()
    weight_pair().start()
    pltpu.make_async_copy(w_ref.at[:, :, weight_cols(head)], weights.at[z, core], w_sem.at[z, core]).start()

    scale = math.log2(math.e) / math.sqrt(HD)
    hh = heads * place_x + place_y

    def share(block):
        span = pl.ds(pl.multiple_of(core * part, 128), part)
        return pltpu.make_async_remote_copy(
            src_ref=kv_in.at[block, :, span], dst_ref=kv_in.at[block, :, span],
            send_sem=share_send.at[block], recv_sem=share_sem.at[block],
            device_id=sibling, device_id_type=MESH,
        )

    def shared(block):
        span = pl.ds(pl.multiple_of(other * part, 128), part)
        return pltpu.make_async_copy(
            kv_in.at[block, :, span], kv_in.at[block, :, span], share_sem.at[block]
        )

    def mixed_target(block):
        return gathered.at[
            z, pl.ds(pl.multiple_of(core * part, 128), part), pl.ds(pl.multiple_of(hh * HD, 128), HD)
        ]

    def mixed_copy(block):
        return pltpu.make_async_remote_copy(
            src_ref=mixed.at[block], dst_ref=mixed_target(block),
            send_sem=mixed_send.at[block], recv_sem=mixed_sem.at[hh],
            device_id=(first + block, head), device_id_type=MESH,
        )

    tile, group = part // 2, 16
    chunks = rows // HD

    def attend(pairs):
        tiles = [(pair, t) for pair in pairs for t in range(part // tile)]

        def score(n):
            (q_block, k_block, _), t = tiles[n]
            scores[n][...] = jnp.dot(
                q_two[q_block, pl.ds(t * tile, tile)], keys_across[k_block], preferred_element_type=jnp.float32
            )

        def soften(n):
            (q_block, k_block, diagonal), t = tiles[n]
            spans = [pl.ds(t * tile + g * group, group) for g in range(tile // group)]
            bounds = [low[q_block, span] - k_block * rows for span in spans]
            olds = [top[q_block, span] for span in spans]
            news = []
            for g, (bound, old) in enumerate(zip(bounds, olds)):
                parts = []
                for m in range(chunks):
                    lanes = lax.broadcasted_iota(jnp.int32, (group, HD), 1) + m * HD
                    allowed = lanes >= bound
                    if diagonal:
                        first_row = core * part + (t * tile + g * group)
                        allowed &= lanes <= lax.broadcasted_iota(jnp.int32, (group, HD), 0) + first_row
                    parts.append(jnp.where(allowed, scores[n][pl.ds(g * group, group), pl.ds(m * HD, HD)], MASKED))
                most = functools.reduce(jnp.maximum, parts)
                new = jnp.maximum(old, jnp.max(most, axis=1, keepdims=True))
                news.append(new)
                for m in range(chunks):
                    shares[n][pl.ds(g * group, group), pl.ds(m * HD, HD)] = jnp.exp2(parts[m] - new).astype(
                        jnp.bfloat16
                    )
            for span, new in zip(spans, news):
                top[q_block, span] = new
            return spans, olds, news

        def mix(n, state):
            (q_block, k_block, _), t = tiles[n]
            values = kv_in[k_block, 1]
            values = jnp.concatenate([values, jnp.ones_like(values)], axis=1)
            product = jnp.dot(shares[n][...], values, preferred_element_type=jnp.float32)
            factors = [jnp.exp2(old - new) for _, old, new in zip(*state)]
            sums = [
                accum[q_block, span] * jnp.concatenate([factor, factor], axis=1)
                for span, factor in zip(state[0], factors)
            ]
            for g, span in enumerate(state[0]):
                accum[q_block, span] = sums[g] + product[g * group : (g + 1) * group]

        score(0)
        for n in range(len(tiles)):
            if n + 1 < len(tiles):
                score(n + 1)
            mix(n, soften(n))

    @pl.when(works)
    def _():
        def blank(block, carry):
            positions = (
                lax.broadcasted_iota(jnp.int32, (part, HD), 0) + (half * BLOCKS + block) * rows + core * part
            )
            start = jnp.zeros((part, HD), jnp.int32)
            end = jnp.int32(0)
            for doc in range(lengths_ref.shape[0]):
                end = end + lengths_ref[doc]
                start = jnp.where(positions >= end, end, start)
            low[block] = start - half * BLOCKS * rows
            top[block] = jnp.full((part, HD), FLOOR, jnp.float32)
            accum[block] = jnp.zeros((part, 2 * HD), jnp.float32)
            return carry

        lax.fori_loop(0, BLOCKS, blank, 0)

        def block_at(step):
            dx = jnp.where((step == 3) | (step == 4) | (step == 5) | (step == 7), 1, 0)
            dy = jnp.where(
                (step == 1) | (step == 4), 1, jnp.where((step == 2) | (step == 5), 3, jnp.where(step >= 6, 2, 0))
            )
            return lax.rem(place_x + dx, 2) * RING + lax.rem(place_y + dy, RING)

        def receive(step):
            block = block_at(step)
            span = pl.ds(pl.multiple_of(core * part, 128), part)
            arrived = kv_in.at[block, :, span]
            pltpu.make_async_copy(arrived, arrived, kv_sem.at[block]).wait()
            share(block).start()

        ahead = BLOCKS - 2
        receive(0)

        def take(step, carry):
            for late, away in zip(range(BLOCKS - 3, BLOCKS), (1, 3, 2)):
                @pl.when(step == late)
                def _():
                    hand_across(away)

            @pl.when(step < ahead)
            def _():
                receive(step + 1)

            @pl.when(step > ahead)
            def _():
                receive(step)

            block = block_at(step)
            pltpu.make_async_copy(q_in.at[block], q_in.at[block], q_sem.at[block]).wait()
            scaled = q_in[block].astype(jnp.float32) * scale
            upper = scaled.astype(jnp.bfloat16)
            lower = (scaled - upper.astype(jnp.float32)).astype(jnp.bfloat16)
            q_two[block] = jnp.concatenate([upper, lower], axis=1)
            shared(block).wait()
            across = kv_in[block, 0].T
            keys_across[block] = jnp.concatenate([across, across], axis=0)

            def with_past(before):
                past = block_at(before)
                return jnp.maximum(block, past), jnp.minimum(block, past), False

            def two_at_once(count, inner):
                attend([with_past(2 * count), with_past(2 * count + 1)])
                return inner

            lax.fori_loop(0, step // 2, two_at_once, 0)

            @pl.when(lax.rem(step, 2) == 1)
            def _():
                attend([with_past(step - 1), (block, block, True)])

            @pl.when(lax.rem(step, 2) == 0)
            def _():
                attend([(block, block, True)])
            return carry

        lax.fori_loop(0, BLOCKS, take, 0)

        def finish(count, carry):
            block = block_at(BLOCKS - 1 - count)
            result = accum[block]
            mixed[block] = (result[:, :HD] / result[:, HD:]).astype(jnp.bfloat16)

            @pl.when(block == place)
            def _():
                pltpu.make_async_copy(mixed.at[block], mixed_target(block), mixed_sem.at[hh]).start()

            @pl.when(block != place)
            def _():
                mixed_copy(block).start()
            return carry

        lax.fori_loop(0, BLOCKS, finish, 0)

    @pl.when(jnp.logical_not(works))
    def _():
        for away in (1, 3, 2):
            hand_across(away)

    mine = pl.ds(pl.multiple_of(core * part, 128), part)
    theirs = pl.ds(pl.multiple_of(other * part, 128), part)
    halfway = part // 2
    lower_rows = pl.ds(pl.multiple_of(core * part, 128), halfway)
    upper_rows = pl.ds(pl.multiple_of(core * part + halfway, 128), halfway)

    order = [(dx, dy) for dy in (2, 1, 3, 0) for dx in (1, 0)]

    def each(action):
        for dx, dy in order:
            row, local = lax.rem(place_x + dx, 2), lax.rem(place_y + dy, RING)

            @pl.when(local < heads)
            def _():
                action(heads * row + local)

    def piece_of(source, span, piece):
        return gathered.at[source, span, pl.ds(pl.multiple_of(piece * HD, HD), HD)]

    def ring(source, span, piece, target, send, recv):
        return pltpu.make_async_remote_copy(
            src_ref=piece_of(source, span, piece), dst_ref=piece_of(source, span, piece),
            send_sem=send.at[piece], recv_sem=recv.at[piece],
            device_id=(ctx, target * 2 + core), device_id_type=MESH,
        )

    def to_pair(source, piece):
        return pltpu.make_async_remote_copy(
            src_ref=piece_of(source, mine, piece), dst_ref=piece_of(source, mine, piece),
            send_sem=pair_send.at[source, piece], recv_sem=pair_sem.at[source],
            device_id=sibling, device_id_type=MESH,
        )

    def piece_landed(source, span, piece, sem):
        here = piece_of(source, span, piece)
        pltpu.make_async_copy(here, here, sem.at[piece]).wait()

    def up(piece):
        return ring(z, mine, piece, z_up, ring_send.at[0], ring_sem.at[0])

    def down(piece):
        return ring(z, mine, piece, z_down, ring_send.at[1], ring_sem.at[1])

    def relay_up(piece):
        return ring(z_down, lower_rows, piece, z_up, relay_send.at[0], relay_sem.at[0])

    def relay_down(piece):
        return ring(z_up, upper_rows, piece, z_down, relay_send.at[1], relay_sem.at[1])

    def landed(source, span, sem):
        return pltpu.make_async_copy(gathered.at[source, span], gathered.at[source, span], sem)

    def project(away, start, last):
        source = lax.rem(z + away, RING)
        landed(source, theirs, pair_sem.at[source]).wait()
        weights_here(away)
        tile = rows // 4

        def some_rows(n, carry):
            span = pl.ds(pl.multiple_of(n * tile, 128), tile)
            product = jnp.dot(gathered[source, span], weights[source].reshape(2 * width, out_cols), preferred_element_type=jnp.float32)
            if not start:
                product = product + total[span]
            if last:
                out_ref[span] = product.astype(jnp.bfloat16)
            else:
                total[span] = product
            return carry

        lax.fori_loop(0, 4, some_rows, 0)

    def send_own(piece):
        piece_landed(z, mine, piece, mixed_sem)
        up(piece).start()
        down(piece).start()
        to_pair(z, piece).start()

    def pass_on(piece):
        piece_landed(z_down, mine, piece, ring_sem.at[0])
        relay_up(piece).start()
        to_pair(z_down, piece).start()
        piece_landed(z_up, mine, piece, ring_sem.at[1])
        relay_down(piece).start()
        to_pair(z_up, piece).start()

    def take_far(piece):
        piece_landed(z_far, lower_rows, piece, relay_sem.at[0])
        piece_landed(z_far, upper_rows, piece, relay_sem.at[1])
        to_pair(z_far, piece).start()

    each(send_own)
    project(0, True, False)
    each(pass_on)
    project(3, False, False)
    project(1, False, False)
    each(take_far)
    project(2, False, True)

    def all_left(piece):
        for copy in (up(piece), down(piece), relay_up(piece), relay_down(piece)):
            copy.wait_send()
        for source in range(RING):
            to_pair(source, piece).wait_send()

    each(all_left)
    for away in (2, 1, 3):
        for c in range(2):
            weight_copy(away, c).wait_send()
        weight_across(away).wait_send()
    weight_pair().wait_send()
    for group in sends:
        for _, finish in group:
            finish()

    @pl.when(works)
    def _():
        def left(block, carry):
            share(block).wait_send()

            @pl.when(block != place)
            def _():
                mixed_copy(block).wait_send()
            return carry

        lax.fori_loop(0, BLOCKS, left, 0)


def per_device(query, keys, values, doc_lengths, w_out):
    rows, width = query.shape
    heads = width // HD
    part = rows // 2
    out_cols = w_out.shape[1] // lax.axis_size("head")
    dma = pltpu.SemaphoreType.DMA
    pairs = BLOCKS * (BLOCKS + 1) // 2
    flops = pairs * part * rows * 4 * HD + 2 * rows * w_out.shape[1] * width
    return pl.pallas_call(
        kernel,
        out_shape=jax.ShapeDtypeStruct((rows, out_cols), jnp.bfloat16),
        in_specs=[pl.BlockSpec(memory_space=pltpu.SMEM)] + [pl.BlockSpec(memory_space=pl.ANY)] * 4,
        out_specs=pl.BlockSpec(memory_space=pltpu.VMEM),
        scratch_shapes=[
            pltpu.VMEM((BLOCKS, part, HD), jnp.bfloat16),
            pltpu.VMEM((BLOCKS, 2, rows, HD), jnp.bfloat16),
            pltpu.VMEM((BLOCKS, part, 2 * HD), jnp.bfloat16),
            pltpu.VMEM((BLOCKS, 2 * HD, rows), jnp.bfloat16),
            pltpu.VMEM((BLOCKS, part, HD), jnp.int32),
            pltpu.VMEM((BLOCKS, part, HD), jnp.float32),
            pltpu.VMEM((BLOCKS, part, 2 * HD), jnp.float32),
            [pltpu.VMEM((part // 2, rows), jnp.float32)] * 4,
            [pltpu.VMEM((part // 2, rows), jnp.bfloat16)] * 4,
            pltpu.VMEM((BLOCKS, part, HD), jnp.bfloat16),
            pltpu.VMEM((RING, rows, 2 * width), jnp.bfloat16),
            pltpu.VMEM((RING, 2, 2, width // 2, out_cols), jnp.bfloat16),
            pltpu.VMEM((rows, out_cols), jnp.float32),
            dma((RING, 2, 3)),
            dma((BLOCKS,)),
            dma((BLOCKS,)),
            dma((BLOCKS,)),
            dma((BLOCKS,)),
            dma((BLOCKS,)),
            dma((2 * heads,)),
            dma((RING, 2)),
            dma((RING, 2)),
            dma((RING,)),
            dma((RING,)),
            dma((2, 2 * heads)),
            dma((2, 2 * heads)),
            dma((2, 2 * heads)),
            dma((2, 2 * heads)),
            dma((RING, 2 * heads)),
            dma((RING,)),
        ],
        compiler_params=pltpu.CompilerParams(
            collective_id=0, has_side_effects=True, vmem_limit_bytes=56 * 1024 * 1024
        ),
        cost_estimate=pl.CostEstimate(
            flops=flops, bytes_accessed=16 * 1024 * 1024, transcendentals=pairs * part * rows
        ),
    )(doc_lengths, query, keys, values, w_out.reshape(2, width // 2, w_out.shape[1]))


def solution(mesh):
    return jax.shard_map(
        per_device,
        mesh=mesh,
        in_specs=(P("ctx", "head"), P("ctx", "head"), P("ctx", "head"), P(), P("head", None)),
        out_specs=P("ctx", "head"),
        check_vma=False,
    )
```

time: 661 us -> 123 us (0.19)
  waiting for transfers between devices: 418 us -> 0 us
  Pallas kernels: 0 us -> 120 us
  starting transfers between devices: 81.4 us -> 0 us
  local copies, waits for them, and re-layouts: 78 us -> 2.49 us
  loops' own time: 37.6 us -> 0 us
  matrix products: 20.9 us -> 0 us
  between operations: 16 us -> 0.01 us
  other arithmetic: 7.05 us -> 0 us
    ppermute x15 -> x0, waiting for transfers between devices: 330 us -> none  [passed_along(): return lax.ppermute(value, axis, pairs)]
    pallas_call x0 -> x1, Pallas kernels: none -> 120 us  [per_device(): pl.pallas_call(kernel, out_shape=jax.ShapeDtypeStruct((rows, out_cols), j...]
    unnamed x2 -> x0, waiting for transfers between devices: 87.6 us -> none
    ppermute x15 -> x0, starting transfers between devices: 81.4 us -> none  [passed_along(): return lax.ppermute(value, axis, pairs)]
    another operation x17 -> x0, loops' own time: 37.6 us -> none  [the longest x1 37.1 us: per_device(): kv_now, states = lax.fori_loop(0, reach, pass_far, (kv_local, states))]
    slice x64 -> x0, local copies, waits for them, and re-layouts: 36.9 us -> none  [visit(): masked = (key_pos[0] > query_pos[-1]) | (key_doc[-1] < query_doc[0])]
    dot_general x3 -> x0, matrix products: 20.9 us -> none  [the longest x1 10.2 us: per_device(): projected = jnp.dot(attended, w_out, preferred_element_type=jnp.float32)]
    unnamed x9 -> x1, local copies, waits for them, and re-layouts: 23.1 us -> 2.49 us
  transfers between devices with their start and end apart: 16 -> 0, of which waited for: 16 -> 0; matrix products, arithmetic and copies ran while one was open for 8% -> 0% of each run, Pallas kernels for 0% -> 0%
where the time goes in v1:
time: 123 us; the launch traced here: 122 us
  Pallas kernels  120 us (98%)
  local copies, waits for them, and re-layouts  2.49 us (2%)
    pallas_call x1, Pallas kernels, per_device(): pl.pallas_call(kernel, out_shape=jax.ShapeDtypeStruct((rows, out_cols), j...  120 us
    unnamed x1, local copies, waits for them, and re-layouts  2.49 us

profile of v1, /device:TPU:1, one launch (start us, length us, event | category | flops | bytes accessed | tf_op | source)
XLA Modules:
  0.0 122.1 jit_solution(5976222795010777002)
XLA Ops:
  0.0 119.6 %shard_map.55 = bf16[1024,640]{1,0:T(8,128)(2,1)} custom-call(s32[8]{0:T(128)} %lengths_ref.1, bf16[1024,384]{1,0:T(8,128)(2,1)} %q_ref.1, bf16[1024,384]{1,0:T(8,128)(2,1)} %k_ref.1, bf16[1024,384]{1,0:T(8,128)(2,1)} %v_ref.1, bf16[2,192,5120]{2,1,0:T(8,128)(2,1)} %bitcast.1), custom_call_target="tpu_custom_call" | custom-call | flops 13690208256 | bytes 16777216 | tf_op jit(solution)/shard_map/pallas_call | solution.py:473
  119.6 2.5 %copy.7 = bf16[1024,640]{1,0:T(8,128)(2,1)} copy(bf16[1024,640]{1,0:T(8,128)(2,1)} %shard_map.55) | data formatting | bytes 2621440

commit v2 on v1

--- a/solution.py
+++ b/solution.py
@@ -11,14 +11,14 @@
 HD = 128
 BLOCKS = 8
 RING = 4
-MASKED = -1e30
-FLOOR = -1e29
+OTHER_DOC = -(2.0**20)
+FLOOR = -5e5
 MESH = pl.DeviceIdType.MESH
 
 
 def kernel(
     lengths_ref, q_ref, k_ref, v_ref, w_ref, out_ref,
-    q_in, kv_in, q_two, keys_across, low, top, accum, scores, shares, mixed, gathered, weights, total,
+    q_in, kv_in, q_two, keys_across, top, accum, scores, shares, mixed, gathered, weights, total,
     send_sem, q_sem, kv_sem, share_send, share_sem, mixed_send, mixed_sem,
     w_send, w_sem, across_send, across_sem, ring_send, ring_sem, relay_send, relay_sem, pair_send, pair_sem,
 ):
@@ -177,7 +177,7 @@
             device_id=(first + block, head), device_id_type=MESH,
         )
 
-    tile, group = part // 2, 16
+    tile, group = part, 16
     chunks = rows // HD
 
     def attend(pairs):
@@ -192,23 +192,23 @@
         def soften(n):
             (q_block, k_block, diagonal), t = tiles[n]
             spans = [pl.ds(t * tile + g * group, group) for g in range(tile // group)]
-            bounds = [low[q_block, span] - k_block * rows for span in spans]
             olds = [top[q_block, span] for span in spans]
             news = []
-            for g, (bound, old) in enumerate(zip(bounds, olds)):
+            for g, old in enumerate(olds):
                 parts = []
                 for m in range(chunks):
-                    lanes = lax.broadcasted_iota(jnp.int32, (group, HD), 1) + m * HD
-                    allowed = lanes >= bound
+                    piece = scores[n][pl.ds(g * group, group), pl.ds(m * HD, HD)]
                     if diagonal:
+                        lanes = lax.broadcasted_iota(jnp.int32, (group, HD), 1) + m * HD
                         first_row = core * part + (t * tile + g * group)
-                        allowed &= lanes <= lax.broadcasted_iota(jnp.int32, (group, HD), 0) + first_row
-                    parts.append(jnp.where(allowed, scores[n][pl.ds(g * group, group), pl.ds(m * HD, HD)], MASKED))
+                        allowed = lanes <= lax.broadcasted_iota(jnp.int32, (group, HD), 0) + first_row
+                        piece = jnp.where(allowed, piece, OTHER_DOC)
+                    parts.append(piece)
                 most = functools.reduce(jnp.maximum, parts)
                 new = jnp.maximum(old, jnp.max(most, axis=1, keepdims=True))
                 news.append(new)
                 for m in range(chunks):
-                    shares[n][pl.ds(g * group, group), pl.ds(m * HD, HD)] = jnp.exp2(parts[m] - new).astype(
+                    shares[n][pl.ds(g * group, group), pl.ds(m * HD, HD)] = jnp.exp2((parts[m] - new) * scale).astype(
                         jnp.bfloat16
                     )
             for span, new in zip(spans, news):
@@ -220,7 +220,7 @@
             values = kv_in[k_block, 1]
             values = jnp.concatenate([values, jnp.ones_like(values)], axis=1)
             product = jnp.dot(shares[n][...], values, preferred_element_type=jnp.float32)
-            factors = [jnp.exp2(old - new) for _, old, new in zip(*state)]
+            factors = [jnp.exp2((old - new) * scale) for _, old, new in zip(*state)]
             sums = [
                 accum[q_block, span] * jnp.concatenate([factor, factor], axis=1)
                 for span, factor in zip(state[0], factors)
@@ -236,16 +236,21 @@
 
     @pl.when(works)
     def _():
+        def doc_at(positions):
+            doc, end = jnp.zeros_like(positions), jnp.int32(0)
+            for n in range(lengths_ref.shape[0]):
+                end = end + lengths_ref[n]
+                doc = jnp.where(positions >= end, n + 1, doc)
+            return doc
+
         def blank(block, carry):
-            positions = (
-                lax.broadcasted_iota(jnp.int32, (part, HD), 0) + (half * BLOCKS + block) * rows + core * part
-            )
-            start = jnp.zeros((part, HD), jnp.int32)
-            end = jnp.int32(0)
-            for doc in range(lengths_ref.shape[0]):
-                end = end + lengths_ref[doc]
-                start = jnp.where(positions >= end, end, start)
-            low[block] = start - half * BLOCKS * rows
+            start = (half * BLOCKS + block) * rows
+            q_doc = doc_at(lax.broadcasted_iota(jnp.int32, (part, HD), 0) + (start + core * part))
+            same = lax.broadcasted_iota(jnp.int32, (part, HD), 1) == q_doc
+            q_two[block, :, pl.ds(HD, HD)] = jnp.where(same, 0.0, OTHER_DOC).astype(jnp.bfloat16)
+            k_doc = doc_at(lax.broadcasted_iota(jnp.int32, (HD, rows), 1) + start)
+            same = lax.broadcasted_iota(jnp.int32, (HD, rows), 0) == k_doc
+            keys_across[block, pl.ds(HD, HD)] = jnp.where(same, 1.0, 0.0).astype(jnp.bfloat16)
             top[block] = jnp.full((part, HD), FLOOR, jnp.float32)
             accum[block] = jnp.zeros((part, 2 * HD), jnp.float32)
             return carry
@@ -285,13 +290,9 @@
 
             block = block_at(step)
             pltpu.make_async_copy(q_in.at[block], q_in.at[block], q_sem.at[block]).wait()
-            scaled = q_in[block].astype(jnp.float32) * scale
-            upper = scaled.astype(jnp.bfloat16)
-            lower = (scaled - upper.astype(jnp.float32)).astype(jnp.bfloat16)
-            q_two[block] = jnp.concatenate([upper, lower], axis=1)
+            q_two[block, :, pl.ds(0, HD)] = q_in[block]
             shared(block).wait()
-            across = kv_in[block, 0].T
-            keys_across[block] = jnp.concatenate([across, across], axis=0)
+            keys_across[block, pl.ds(0, HD)] = kv_in[block, 0].T
 
             def with_past(before):
                 past = block_at(before)
@@ -480,11 +481,10 @@
             pltpu.VMEM((BLOCKS, 2, rows, HD), jnp.bfloat16),
             pltpu.VMEM((BLOCKS, part, 2 * HD), jnp.bfloat16),
             pltpu.VMEM((BLOCKS, 2 * HD, rows), jnp.bfloat16),
-            pltpu.VMEM((BLOCKS, part, HD), jnp.int32),
             pltpu.VMEM((BLOCKS, part, HD), jnp.float32),
             pltpu.VMEM((BLOCKS, part, 2 * HD), jnp.float32),
-            [pltpu.VMEM((part // 2, rows), jnp.float32)] * 4,
-            [pltpu.VMEM((part // 2, rows), jnp.bfloat16)] * 4,
+            [pltpu.VMEM((part, rows), jnp.float32)] * 2,
+            [pltpu.VMEM((part, rows), jnp.bfloat16)] * 2,
             pltpu.VMEM((BLOCKS, part, HD), jnp.bfloat16),
             pltpu.VMEM((RING, rows, 2 * width), jnp.bfloat16),
             pltpu.VMEM((RING, 2, 2, width // 2, out_cols), jnp.bfloat16),

time: 123 us -> 117 us (0.951)
  Pallas kernels: 120 us -> 114 us
    pallas_call x1, Pallas kernels: 120 us -> 114 us  [per_device(): pl.pallas_call(kernel, out_shape=jax.ShapeDtypeStruct((rows, out_cols), j...]
where the time goes in v2:
time: 117 us; the launch traced here: 116 us
  Pallas kernels  114 us (97%)
  local copies, waits for them, and re-layouts  2.49 us (2%)
    pallas_call x1, Pallas kernels, per_device(): pl.pallas_call(kernel, out_shape=jax.ShapeDtypeStruct((rows, out_cols), j...  114 us
    unnamed x1, local copies, waits for them, and re-layouts  2.49 us

profile of v2, /device:TPU:1, one launch (start us, length us, event | category | flops | bytes accessed | tf_op | source)
XLA Modules:
  0.0 116.5 jit_solution(5852599756101934920)
XLA Ops:
  0.0 114.0 %shard_map.55 = bf16[1024,640]{1,0:T(8,128)(2,1)} custom-call(s32[8]{0:T(128)} %lengths_ref.1, bf16[1024,384]{1,0:T(8,128)(2,1)} %q_ref.1, bf16[1024,384]{1,0:T(8,128)(2,1)} %k_ref.1, bf16[1024,384]{1,0:T(8,128)(2,1)} %v_ref.1, bf16[2,192,5120]{2,1,0:T(8,128)(2,1)} %bitcast.1), custom_call_target="tpu_custom_call" | custom-call | flops 13690208256 | bytes 16777216 | tf_op jit(solution)/shard_map/pallas_call | solution.py:474
  114.0 2.5 %copy.7 = bf16[1024,640]{1,0:T(8,128)(2,1)} copy(bf16[1024,640]{1,0:T(8,128)(2,1)} %shard_map.55) | data formatting | bytes 2621440

commit v3 on v2

--- a/solution.py
+++ b/solution.py
@@ -165,33 +165,51 @@
             kv_in.at[block, :, span], kv_in.at[block, :, span], share_sem.at[block]
         )
 
-    def mixed_target(block):
-        return gathered.at[
-            z, pl.ds(pl.multiple_of(core * part, 128), part), pl.ds(pl.multiple_of(hh * HD, 128), HD)
-        ]
-
-    def mixed_copy(block):
-        return pltpu.make_async_remote_copy(
-            src_ref=mixed.at[block], dst_ref=mixed_target(block),
-            send_sem=mixed_send.at[block], recv_sem=mixed_sem.at[hh],
+    tile, group = part // 2, 16
+    chunks = rows // HD
+
+    def half_rows(c, t):
+        return pl.ds(pl.multiple_of(c * part + t * tile, 128), tile)
+
+    def mixed_target(t):
+        return gathered.at[z, half_rows(core, t), pl.ds(pl.multiple_of(hh * HD, HD), HD)]
+
+    def mixed_source(block, t):
+        return mixed.at[block, pl.ds(pl.multiple_of(t * tile, 128), tile)]
+
+    def mixed_copy(block, t):
+        return pltpu.make_async_remote_copy(
+            src_ref=mixed_source(block, t), dst_ref=mixed_target(t),
+            send_sem=mixed_send.at[t, block], recv_sem=mixed_sem.at[t, hh],
             device_id=(first + block, head), device_id_type=MESH,
         )
 
-    tile, group = part, 16
-    chunks = rows // HD
-
-    def attend(pairs):
-        tiles = [(pair, t) for pair in pairs for t in range(part // tile)]
+    def finish(block, t):
+        result = accum[block, pl.ds(pl.multiple_of(t * tile, 128), tile)]
+        mixed[block, pl.ds(pl.multiple_of(t * tile, 128), tile)] = (
+            result[:, :HD] / result[:, HD:]
+        ).astype(jnp.bfloat16)
+
+        @pl.when(block == place)
+        def _():
+            pltpu.make_async_copy(mixed_source(block, t), mixed_target(t), mixed_sem.at[t, hh]).start()
+
+        @pl.when(block != place)
+        def _():
+            mixed_copy(block, t).start()
+
+    def attend(tiles, t):
+        first_row = pl.multiple_of(t * tile, 128)
 
         def score(n):
-            (q_block, k_block, _), t = tiles[n]
+            q_block, k_block, _ = tiles[n]
             scores[n][...] = jnp.dot(
-                q_two[q_block, pl.ds(t * tile, tile)], keys_across[k_block], preferred_element_type=jnp.float32
+                q_two[q_block, pl.ds(first_row, tile)], keys_across[k_block], preferred_element_type=jnp.float32
             )
 
         def soften(n):
-            (q_block, k_block, diagonal), t = tiles[n]
-            spans = [pl.ds(t * tile + g * group, group) for g in range(tile // group)]
+            q_block, k_block, diagonal = tiles[n]
+            spans = [pl.ds(pl.multiple_of(first_row + g * group, group), group) for g in range(tile // group)]
             olds = [top[q_block, span] for span in spans]
             news = []
             for g, old in enumerate(olds):
@@ -200,8 +218,8 @@
                     piece = scores[n][pl.ds(g * group, group), pl.ds(m * HD, HD)]
                     if diagonal:
                         lanes = lax.broadcasted_iota(jnp.int32, (group, HD), 1) + m * HD
-                        first_row = core * part + (t * tile + g * group)
-                        allowed = lanes <= lax.broadcasted_iota(jnp.int32, (group, HD), 0) + first_row
+                        row = core * part + first_row + g * group
+                        allowed = lanes <= lax.broadcasted_iota(jnp.int32, (group, HD), 0) + row
                         piece = jnp.where(allowed, piece, OTHER_DOC)
                     parts.append(piece)
                 most = functools.reduce(jnp.maximum, parts)
@@ -216,7 +234,7 @@
             return spans, olds, news
 
         def mix(n, state):
-            (q_block, k_block, _), t = tiles[n]
+            q_block, k_block, _ = tiles[n]
             values = kv_in[k_block, 1]
             values = jnp.concatenate([values, jnp.ones_like(values)], axis=1)
             product = jnp.dot(shares[n][...], values, preferred_element_type=jnp.float32)
@@ -233,6 +251,75 @@
             if n + 1 < len(tiles):
                 score(n + 1)
             mix(n, soften(n))
+
+    order = [(dx, dy) for dy in (2, 1, 3, 0) for dx in (1, 0)]
+
+    def each(action, t):
+        for dx, dy in order:
+            row, local = lax.rem(place_x + dx, 2), lax.rem(place_y + dy, RING)
+
+            @pl.when(local < heads)
+            def _():
+                action(heads * row + local, t)
+
+    mine = [half_rows(core, t) for t in range(2)]
+    theirs = [half_rows(other, t) for t in range(2)]
+    far_rows = [
+        [pl.ds(pl.multiple_of(core * part + t * tile + n * (tile // 2), 128), tile // 2) for n in range(2)]
+        for t in range(2)
+    ]
+
+    def piece_of(source, span, piece):
+        return gathered.at[source, span, pl.ds(pl.multiple_of(piece * HD, HD), HD)]
+
+    def ring(source, span, piece, target, send, recv):
+        return pltpu.make_async_remote_copy(
+            src_ref=piece_of(source, span, piece), dst_ref=piece_of(source, span, piece),
+            send_sem=send.at[piece], recv_sem=recv.at[piece],
+            device_id=(ctx, target * 2 + core), device_id_type=MESH,
+        )
+
+    def to_pair(source, piece, t):
+        return pltpu.make_async_remote_copy(
+            src_ref=piece_of(source, mine[t], piece), dst_ref=piece_of(source, mine[t], piece),
+            send_sem=pair_send.at[t, source, piece], recv_sem=pair_sem.at[t, source],
+            device_id=sibling, device_id_type=MESH,
+        )
+
+    def piece_landed(source, span, piece, sem):
+        here = piece_of(source, span, piece)
+        pltpu.make_async_copy(here, here, sem.at[piece]).wait()
+
+    def up(piece, t):
+        return ring(z, mine[t], piece, z_up, ring_send.at[t, 0], ring_sem.at[t, 0])
+
+    def down(piece, t):
+        return ring(z, mine[t], piece, z_down, ring_send.at[t, 1], ring_sem.at[t, 1])
+
+    def relay_up(piece, t):
+        return ring(z_down, far_rows[t][0], piece, z_up, relay_send.at[t, 0], relay_sem.at[t, 0])
+
+    def relay_down(piece, t):
+        return ring(z_up, far_rows[t][1], piece, z_down, relay_send.at[t, 1], relay_sem.at[t, 1])
+
+    def send_own(piece, t):
+        piece_landed(z, mine[t], piece, mixed_sem.at[t])
+        up(piece, t).start()
+        down(piece, t).start()
+        to_pair(z, piece, t).start()
+
+    def pass_on(piece, t):
+        piece_landed(z_down, mine[t], piece, ring_sem.at[t, 0])
+        relay_up(piece, t).start()
+        to_pair(z_down, piece, t).start()
+        piece_landed(z_up, mine[t], piece, ring_sem.at[t, 1])
+        relay_down(piece, t).start()
+        to_pair(z_up, piece, t).start()
+
+    def take_far(piece, t):
+        piece_landed(z_far, far_rows[t][0], piece, relay_sem.at[t, 0])
+        piece_landed(z_far, far_rows[t][1], piece, relay_sem.at[t, 1])
+        to_pair(z_far, piece, t).start()
 
     @pl.when(works)
     def _():
@@ -274,173 +361,117 @@
         ahead = BLOCKS - 2
         receive(0)
 
-        def take(step, carry):
+        def take(turn, carry):
+            t, step = turn // BLOCKS, lax.rem(turn, BLOCKS)
             for late, away in zip(range(BLOCKS - 3, BLOCKS), (1, 3, 2)):
-                @pl.when(step == late)
+                @pl.when(turn == late)
                 def _():
                     hand_across(away)
 
-            @pl.when(step < ahead)
-            def _():
-                receive(step + 1)
-
-            @pl.when(step > ahead)
-            def _():
-                receive(step)
-
-            block = block_at(step)
-            pltpu.make_async_copy(q_in.at[block], q_in.at[block], q_sem.at[block]).wait()
-            q_two[block, :, pl.ds(0, HD)] = q_in[block]
-            shared(block).wait()
-            keys_across[block, pl.ds(0, HD)] = kv_in[block, 0].T
+            @pl.when(turn < ahead)
+            def _():
+                receive(turn + 1)
+
+            @pl.when((turn > ahead) & (turn < BLOCKS))
+            def _():
+                receive(turn)
+
+            block = jnp.where(t == 0, block_at(step), step)
+
+            @pl.when(t == 0)
+            def _():
+                pltpu.make_async_copy(q_in.at[block], q_in.at[block], q_sem.at[block]).wait()
+                q_two[block, :, pl.ds(0, HD)] = q_in[block]
+                shared(block).wait()
+                keys_across[block, pl.ds(0, HD)] = kv_in[block, 0].T
 
             def with_past(before):
-                past = block_at(before)
+                past = jnp.where(t == 0, block_at(before), before)
                 return jnp.maximum(block, past), jnp.minimum(block, past), False
 
-            def two_at_once(count, inner):
-                attend([with_past(2 * count), with_past(2 * count + 1)])
+            def four_at_once(count, inner):
+                attend([with_past(4 * count + n) for n in range(4)], t)
                 return inner
 
-            lax.fori_loop(0, step // 2, two_at_once, 0)
-
-            @pl.when(lax.rem(step, 2) == 1)
-            def _():
-                attend([with_past(step - 1), (block, block, True)])
-
-            @pl.when(lax.rem(step, 2) == 0)
-            def _():
-                attend([(block, block, True)])
+            lax.fori_loop(0, step // 4, four_at_once, 0)
+            for rest in range(4):
+                @pl.when(lax.rem(step, 4) == rest)
+                def _():
+                    attend([with_past(step - 1 - n) for n in range(rest)] + [(block, block, True)], t)
+
+            @pl.when(t == 1)
+            def _():
+                finish(block, 1)
+
+            @pl.when(turn == BLOCKS - 1)
+            def _():
+                def finish_all(count, inner):
+                    finish(block_at(BLOCKS - 1 - count), 0)
+                    return inner
+
+                lax.fori_loop(0, BLOCKS, finish_all, 0)
+
+            for when, action in ((BLOCKS + 3, send_own), (BLOCKS + 5, pass_on), (BLOCKS + 6, take_far)):
+                @pl.when(turn == when)
+                def _():
+                    each(action, 0)
+
             return carry
 
-        lax.fori_loop(0, BLOCKS, take, 0)
-
-        def finish(count, carry):
-            block = block_at(BLOCKS - 1 - count)
-            result = accum[block]
-            mixed[block] = (result[:, :HD] / result[:, HD:]).astype(jnp.bfloat16)
-
-            @pl.when(block == place)
-            def _():
-                pltpu.make_async_copy(mixed.at[block], mixed_target(block), mixed_sem.at[hh]).start()
-
-            @pl.when(block != place)
-            def _():
-                mixed_copy(block).start()
-            return carry
-
-        lax.fori_loop(0, BLOCKS, finish, 0)
+        lax.fori_loop(0, 2 * BLOCKS, take, 0)
 
     @pl.when(jnp.logical_not(works))
     def _():
         for away in (1, 3, 2):
             hand_across(away)
-
-    mine = pl.ds(pl.multiple_of(core * part, 128), part)
-    theirs = pl.ds(pl.multiple_of(other * part, 128), part)
-    halfway = part // 2
-    lower_rows = pl.ds(pl.multiple_of(core * part, 128), halfway)
-    upper_rows = pl.ds(pl.multiple_of(core * part + halfway, 128), halfway)
-
-    order = [(dx, dy) for dy in (2, 1, 3, 0) for dx in (1, 0)]
-
-    def each(action):
-        for dx, dy in order:
-            row, local = lax.rem(place_x + dx, 2), lax.rem(place_y + dy, RING)
-
-            @pl.when(local < heads)
-            def _():
-                action(heads * row + local)
-
-    def piece_of(source, span, piece):
-        return gathered.at[source, span, pl.ds(pl.multiple_of(piece * HD, HD), HD)]
-
-    def ring(source, span, piece, target, send, recv):
-        return pltpu.make_async_remote_copy(
-            src_ref=piece_of(source, span, piece), dst_ref=piece_of(source, span, piece),
-            send_sem=send.at[piece], recv_sem=recv.at[piece],
-            device_id=(ctx, target * 2 + core), device_id_type=MESH,
-        )
-
-    def to_pair(source, piece):
-        return pltpu.make_async_remote_copy(
-            src_ref=piece_of(source, mine, piece), dst_ref=piece_of(source, mine, piece),
-            send_sem=pair_send.at[source, piece], recv_sem=pair_sem.at[source],
-            device_id=sibling, device_id_type=MESH,
-        )
-
-    def piece_landed(source, span, piece, sem):
-        here = piece_of(source, span, piece)
-        pltpu.make_async_copy(here, here, sem.at[piece]).wait()
-
-    def up(piece):
-        return ring(z, mine, piece, z_up, ring_send.at[0], ring_sem.at[0])
-
-    def down(piece):
-        return ring(z, mine, piece, z_down, ring_send.at[1], ring_sem.at[1])
-
-    def relay_up(piece):
-        return ring(z_down, lower_rows, piece, z_up, relay_send.at[0], relay_sem.at[0])
-
-    def relay_down(piece):
-        return ring(z_up, upper_rows, piece, z_down, relay_send.at[1], relay_sem.at[1])
-
-    def landed(source, span, sem):
-        return pltpu.make_async_copy(gathered.at[source, span], gathered.at[source, span], sem)
-
-    def project(away, start, last):
+        for action in (send_own, pass_on, take_far):
+            each(action, 0)
+
+    def half_landed(away, t):
         source = lax.rem(z + away, RING)
-        landed(source, theirs, pair_sem.at[source]).wait()
-        weights_here(away)
-        tile = rows // 4
-
-        def some_rows(n, carry):
-            span = pl.ds(pl.multiple_of(n * tile, 128), tile)
-            product = jnp.dot(gathered[source, span], weights[source].reshape(2 * width, out_cols), preferred_element_type=jnp.float32)
-            if not start:
-                product = product + total[span]
+        here = gathered.at[source, theirs[t]]
+        pltpu.make_async_copy(here, here, pair_sem.at[t, source]).wait()
+
+    def project(aways, t, start, last):
+        def some_rows(c, carry):
+            span = half_rows(c, t)
+            product = None if start else total[pl.ds(pl.multiple_of(c * tile, 128), tile)]
+            for away in aways:
+                source = lax.rem(z + away, RING)
+                term = jnp.dot(
+                    gathered[source, span], weights[source].reshape(2 * width, out_cols),
+                    preferred_element_type=jnp.float32,
+                )
+                product = term if product is None else product + term
             if last:
                 out_ref[span] = product.astype(jnp.bfloat16)
             else:
-                total[span] = product
+                total[pl.ds(pl.multiple_of(c * tile, 128), tile)] = product
             return carry
 
-        lax.fori_loop(0, 4, some_rows, 0)
-
-    def send_own(piece):
-        piece_landed(z, mine, piece, mixed_sem)
-        up(piece).start()
-        down(piece).start()
-        to_pair(z, piece).start()
-
-    def pass_on(piece):
-        piece_landed(z_down, mine, piece, ring_sem.at[0])
-        relay_up(piece).start()
-        to_pair(z_down, piece).start()
-        piece_landed(z_up, mine, piece, ring_sem.at[1])
-        relay_down(piece).start()
-        to_pair(z_up, piece).start()
-
-    def take_far(piece):
-        piece_landed(z_far, lower_rows, piece, relay_sem.at[0])
-        piece_landed(z_far, upper_rows, piece, relay_sem.at[1])
-        to_pair(z_far, piece).start()
-
-    each(send_own)
-    project(0, True, False)
-    each(pass_on)
-    project(3, False, False)
-    project(1, False, False)
-    each(take_far)
-    project(2, False, True)
-
-    def all_left(piece):
-        for copy in (up(piece), down(piece), relay_up(piece), relay_down(piece)):
-            copy.wait_send()
+        lax.fori_loop(0, 2, some_rows, 0)
+
+    each(send_own, 1)
+    for away in range(RING):
+        half_landed(away, 0)
+        weights_here(away)
+    project((0, 1, 2, 3), 0, True, True)
+    each(pass_on, 1)
+    for away in (0, 1, 3):
+        half_landed(away, 1)
+    project((0, 1, 3), 1, True, False)
+    each(take_far, 1)
+    half_landed(2, 1)
+    project((2,), 1, False, True)
+
+    def all_left(piece, t):
+        for copy in (up, down, relay_up, relay_down):
+            copy(piece, t).wait_send()
         for source in range(RING):
-            to_pair(source, piece).wait_send()
-
-    each(all_left)
+            to_pair(source, piece, t).wait_send()
+
+    for t in range(2):
+        each(all_left, t)
     for away in (2, 1, 3):
         for c in range(2):
             weight_copy(away, c).wait_send()
@@ -457,7 +488,8 @@
 
             @pl.when(block != place)
             def _():
-                mixed_copy(block).wait_send()
+                for t in range(2):
+                    mixed_copy(block, t).wait_send()
             return carry
 
         lax.fori_loop(0, BLOCKS, left, 0)
@@ -483,29 +515,29 @@
             pltpu.VMEM((BLOCKS, 2 * HD, rows), jnp.bfloat16),
             pltpu.VMEM((BLOCKS, part, HD), jnp.float32),
             pltpu.VMEM((BLOCKS, part, 2 * HD), jnp.float32),
-            [pltpu.VMEM((part, rows), jnp.float32)] * 2,
-            [pltpu.VMEM((part, rows), jnp.bfloat16)] * 2,
+            [pltpu.VMEM((part // 2, rows), jnp.float32)] * 4,
+            [pltpu.VMEM((part // 2, rows), jnp.bfloat16)] * 4,
             pltpu.VMEM((BLOCKS, part, HD), jnp.bfloat16),
             pltpu.VMEM((RING, rows, 2 * width), jnp.bfloat16),
             pltpu.VMEM((RING, 2, 2, width // 2, out_cols), jnp.bfloat16),
-            pltpu.VMEM((rows, out_cols), jnp.float32),
+            pltpu.VMEM((part, out_cols), jnp.float32),
             dma((RING, 2, 3)),
             dma((BLOCKS,)),
             dma((BLOCKS,)),
             dma((BLOCKS,)),
             dma((BLOCKS,)),
-            dma((BLOCKS,)),
-            dma((2 * heads,)),
+            dma((2, BLOCKS)),
+            dma((2, 2 * heads)),
             dma((RING, 2)),
             dma((RING, 2)),
             dma((RING,)),
             dma((RING,)),
-            dma((2, 2 * heads)),
-            dma((2, 2 * heads)),
-            dma((2, 2 * heads)),
-            dma((2, 2 * heads)),
-            dma((RING, 2 * heads)),
-            dma((RING,)),
+            dma((2, 2, 2 * heads)),
+            dma((2, 2, 2 * heads)),
+            dma((2, 2, 2 * heads)),
+            dma((2, 2, 2 * heads)),
+            dma((2, RING, 2 * heads)),
+            dma((2, RING)),
         ],
         compiler_params=pltpu.CompilerParams(
             collective_id=0, has_side_effects=True, vmem_limit_bytes=56 * 1024 * 1024

time: 117 us -> 110 us (0.940)
  Pallas kernels: 114 us -> 107 us
    pallas_call x1, Pallas kernels: 114 us -> 107 us  [per_device(): pl.pallas_call(kernel, out_shape=jax.ShapeDtypeStruct((rows, out_cols), j...]
where the time goes in v3:
time: 110 us
  Pallas kernels  107 us (97%)
  local copies, waits for them, and re-layouts  2.49 us (2%)
    pallas_call x1, Pallas kernels, per_device(): pl.pallas_call(kernel, out_shape=jax.ShapeDtypeStruct((rows, out_cols), j...  107 us
    unnamed x1, local copies, waits for them, and re-layouts  2.49 us

profile of v3, /device:TPU:1, one launch (start us, length us, event | category | flops | bytes accessed | tf_op | source)
XLA Modules:
  0.0 109.9 jit_solution(10654756433544882152)
XLA Ops:
  0.0 107.4 %shard_map.55 = bf16[1024,640]{1,0:T(8,128)(2,1)} custom-call(s32[8]{0:T(128)} %lengths_ref.1, bf16[1024,384]{1,0:T(8,128)(2,1)} %q_ref.1, bf16[1024,384]{1,0:T(8,128)(2,1)} %k_ref.1, bf16[1024,384]{1,0:T(8,128)(2,1)} %v_ref.1, bf16[2,192,5120]{2,1,0:T(8,128)(2,1)} %bitcast.1), custom_call_target="tpu_custom_call" | custom-call | flops 13690208256 | bytes 16777216 | tf_op jit(solution)/shard_map/pallas_call | solution.py:506
  107.4 2.5 %copy.7 = bf16[1024,640]{1,0:T(8,128)(2,1)} copy(bf16[1024,640]{1,0:T(8,128)(2,1)} %shard_map.55) | data formatting | bytes 2621440

commit v4 on v3

--- a/solution.py
+++ b/solution.py
@@ -208,43 +208,35 @@
             )
 
         def soften(n):
-            q_block, k_block, diagonal = tiles[n]
-            spans = [pl.ds(pl.multiple_of(first_row + g * group, group), group) for g in range(tile // group)]
-            olds = [top[q_block, span] for span in spans]
+            q_block, _, diagonal = tiles[n]
+            rows_here = pl.ds(first_row, tile)
+            old = top[q_block, rows_here]
             news = []
-            for g, old in enumerate(olds):
-                parts = []
-                for m in range(chunks):
-                    piece = scores[n][pl.ds(g * group, group), pl.ds(m * HD, HD)]
-                    if diagonal:
-                        lanes = lax.broadcasted_iota(jnp.int32, (group, HD), 1) + m * HD
-                        row = core * part + first_row + g * group
-                        allowed = lanes <= lax.broadcasted_iota(jnp.int32, (group, HD), 0) + row
-                        piece = jnp.where(allowed, piece, OTHER_DOC)
-                    parts.append(piece)
+            for g in range(tile // group):
+                piece = scores[n][pl.ds(g * group, group)]
+                parts = [piece[:, m * HD : (m + 1) * HD] for m in range(chunks)]
+                if diagonal:
+                    row = core * part + first_row + g * group
+                    row = lax.broadcasted_iota(jnp.int32, (group, HD), 0) + row
+                    lanes = lax.broadcasted_iota(jnp.int32, (group, HD), 1)
+                    parts = [jnp.where(lanes + m * HD <= row, one, OTHER_DOC) for m, one in enumerate(parts)]
                 most = functools.reduce(jnp.maximum, parts)
-                new = jnp.maximum(old, jnp.max(most, axis=1, keepdims=True))
+                new = jnp.maximum(old[g * group : (g + 1) * group], jnp.max(most, axis=1, keepdims=True))
                 news.append(new)
-                for m in range(chunks):
-                    shares[n][pl.ds(g * group, group), pl.ds(m * HD, HD)] = jnp.exp2((parts[m] - new) * scale).astype(
-                        jnp.bfloat16
-                    )
-            for span, new in zip(spans, news):
-                top[q_block, span] = new
-            return spans, olds, news
-
-        def mix(n, state):
+                weight = [jnp.exp2((one - new) * scale).astype(jnp.bfloat16) for one in parts]
+                shares[n][pl.ds(g * group, group)] = jnp.concatenate(weight, axis=1)
+            new = jnp.concatenate(news, axis=0)
+            top[q_block, rows_here] = new
+            return jnp.exp2((old - new) * scale)
+
+        def mix(n, factor):
             q_block, k_block, _ = tiles[n]
+            rows_here = pl.ds(first_row, tile)
             values = kv_in[k_block, 1]
             values = jnp.concatenate([values, jnp.ones_like(values)], axis=1)
             product = jnp.dot(shares[n][...], values, preferred_element_type=jnp.float32)
-            factors = [jnp.exp2((old - new) * scale) for _, old, new in zip(*state)]
-            sums = [
-                accum[q_block, span] * jnp.concatenate([factor, factor], axis=1)
-                for span, factor in zip(state[0], factors)
-            ]
-            for g, span in enumerate(state[0]):
-                accum[q_block, span] = sums[g] + product[g * group : (g + 1) * group]
+            factor = jnp.concatenate([factor, factor], axis=1)
+            accum[q_block, rows_here] = accum[q_block, rows_here] * factor + product
 
         score(0)
         for n in range(len(tiles)):
@@ -323,27 +315,6 @@
 
     @pl.when(works)
     def _():
-        def doc_at(positions):
-            doc, end = jnp.zeros_like(positions), jnp.int32(0)
-            for n in range(lengths_ref.shape[0]):
-                end = end + lengths_ref[n]
-                doc = jnp.where(positions >= end, n + 1, doc)
-            return doc
-
-        def blank(block, carry):
-            start = (half * BLOCKS + block) * rows
-            q_doc = doc_at(lax.broadcasted_iota(jnp.int32, (part, HD), 0) + (start + core * part))
-            same = lax.broadcasted_iota(jnp.int32, (part, HD), 1) == q_doc
-            q_two[block, :, pl.ds(HD, HD)] = jnp.where(same, 0.0, OTHER_DOC).astype(jnp.bfloat16)
-            k_doc = doc_at(lax.broadcasted_iota(jnp.int32, (HD, rows), 1) + start)
-            same = lax.broadcasted_iota(jnp.int32, (HD, rows), 0) == k_doc
-            keys_across[block, pl.ds(HD, HD)] = jnp.where(same, 1.0, 0.0).astype(jnp.bfloat16)
-            top[block] = jnp.full((part, HD), FLOOR, jnp.float32)
-            accum[block] = jnp.zeros((part, 2 * HD), jnp.float32)
-            return carry
-
-        lax.fori_loop(0, BLOCKS, blank, 0)
-
         def block_at(step):
             dx = jnp.where((step == 3) | (step == 4) | (step == 5) | (step == 7), 1, 0)
             dy = jnp.where(
@@ -358,8 +329,41 @@
             pltpu.make_async_copy(arrived, arrived, kv_sem.at[block]).wait()
             share(block).start()
 
+        receive(0)
+
+        def limits(shape, dim):
+            index = lax.broadcasted_iota(jnp.int32, shape, dim)
+            begin, end = jnp.zeros(shape, jnp.int32), jnp.zeros(shape, jnp.int32)
+            last = jnp.int32(0)
+            for n in range(lengths_ref.shape[0]):
+                begin = jnp.where(index == n, last, begin)
+                last = last + lengths_ref[n]
+                end = jnp.where(index == n, last, end)
+            return begin, end
+
+        q_begin, q_end = limits((8, HD), 1)
+        k_begin, k_end = limits((8, HD), 0)
+
+        def blank(block, carry):
+            start = (half * BLOCKS + block) * rows
+            place_q = lax.broadcasted_iota(jnp.int32, (part // 8, 8, HD), 0) * 8
+            place_q = place_q + lax.broadcasted_iota(jnp.int32, (part // 8, 8, HD), 1) + (start + core * part)
+            same = (place_q >= q_begin[None]) & (place_q < q_end[None])
+            lanes_q = jnp.where(same, 0.0, OTHER_DOC).reshape(part, HD)
+            q_two[block, :, pl.ds(HD, HD)] = lanes_q.astype(jnp.bfloat16)
+            for m in range(chunks):
+                place_k = lax.broadcasted_iota(jnp.int32, (8, HD), 1) + (start + m * HD)
+                same = (place_k >= k_begin) & (place_k < k_end)
+                ones = jnp.where(same, 1.0, 0.0)
+                ones = jnp.concatenate([ones, jnp.zeros((HD - 8, HD), jnp.float32)], axis=0)
+                keys_across[block, pl.ds(HD, HD), pl.ds(m * HD, HD)] = ones.astype(jnp.bfloat16)
+            top[block] = jnp.full((part, HD), FLOOR, jnp.float32)
+            accum[block] = jnp.zeros((part, 2 * HD), jnp.float32)
+            return carry
+
+        lax.fori_loop(0, BLOCKS, blank, 0)
+
         ahead = BLOCKS - 2
-        receive(0)
 
         def take(turn, carry):
             t, step = turn // BLOCKS, lax.rem(turn, BLOCKS)
@@ -411,7 +415,7 @@
 
                 lax.fori_loop(0, BLOCKS, finish_all, 0)
 
-            for when, action in ((BLOCKS + 3, send_own), (BLOCKS + 5, pass_on), (BLOCKS + 6, take_far)):
+            for when, action in ((BLOCKS + 5, send_own), (BLOCKS + 6, pass_on), (BLOCKS + 7, take_far)):
                 @pl.when(turn == when)
                 def _():
                     each(action, 0)

time: 110 us -> 110 us (level)
  no operation moved by 1% of the time
where the time goes in v4:
time: 110 us
  Pallas kernels  107 us (97%)
  local copies, waits for them, and re-layouts  2.49 us (2%)
    pallas_call x1, Pallas kernels, per_device(): pl.pallas_call(kernel, out_shape=jax.ShapeDtypeStruct((rows, out_cols), j...  107 us
    unnamed x1, local copies, waits for them, and re-layouts  2.49 us

profile of v4, /device:TPU:1, one launch (start us, length us, event | category | flops | bytes accessed | tf_op | source)
XLA Modules:
  0.0 109.8 jit_solution(8576978536802665779)
XLA Ops:
  0.0 107.3 %shard_map.55 = bf16[1024,640]{1,0:T(8,128)(2,1)} custom-call(s32[8]{0:T(128)} %lengths_ref.1, bf16[1024,384]{1,0:T(8,128)(2,1)} %q_ref.1, bf16[1024,384]{1,0:T(8,128)(2,1)} %k_ref.1, bf16[1024,384]{1,0:T(8,128)(2,1)} %v_ref.1, bf16[2,192,5120]{2,1,0:T(8,128)(2,1)} %bitcast.1), custom_call_target="tpu_custom_call" | custom-call | flops 13690208256 | bytes 16777216 | tf_op jit(solution)/shard_map/pallas_call | solution.py:510
  107.3 2.5 %copy.7 = bf16[1024,640]{1,0:T(8,128)(2,1)} copy(bf16[1024,640]{1,0:T(8,128)(2,1)} %shard_map.55) | data formatting | bytes 2621440

commit v5 on v4

--- a/solution.py
+++ b/solution.py
@@ -165,17 +165,18 @@
             kv_in.at[block, :, span], kv_in.at[block, :, span], share_sem.at[block]
         )
 
-    tile, group = part // 2, 16
+    sizes, group = (part * 3 // 4, part // 4), 16
+    offsets = (0, sizes[0])
     chunks = rows // HD
 
     def half_rows(c, t):
-        return pl.ds(pl.multiple_of(c * part + t * tile, 128), tile)
+        return pl.ds(pl.multiple_of(c * part + offsets[t], 128), sizes[t])
 
     def mixed_target(t):
         return gathered.at[z, half_rows(core, t), pl.ds(pl.multiple_of(hh * HD, HD), HD)]
 
     def mixed_source(block, t):
-        return mixed.at[block, pl.ds(pl.multiple_of(t * tile, 128), tile)]
+        return mixed.at[block, pl.ds(offsets[t], sizes[t])]
 
     def mixed_copy(block, t):
         return pltpu.make_async_remote_copy(
@@ -185,8 +186,8 @@
         )
 
     def finish(block, t):
-        result = accum[block, pl.ds(pl.multiple_of(t * tile, 128), tile)]
-        mixed[block, pl.ds(pl.multiple_of(t * tile, 128), tile)] = (
+        result = accum[block, pl.ds(offsets[t], sizes[t])]
+        mixed[block, pl.ds(offsets[t], sizes[t])] = (
             result[:, :HD] / result[:, HD:]
         ).astype(jnp.bfloat16)
 
@@ -199,11 +200,12 @@
             mixed_copy(block, t).start()
 
     def attend(tiles, t):
-        first_row = pl.multiple_of(t * tile, 128)
+        first_row, tile = offsets[t], sizes[t]
+        score_refs, share_refs = scores[2 * t :], shares[2 * t :]
 
         def score(n):
             q_block, k_block, _ = tiles[n]
-            scores[n][...] = jnp.dot(
+            score_refs[n][...] = jnp.dot(
                 q_two[q_block, pl.ds(first_row, tile)], keys_across[k_block], preferred_element_type=jnp.float32
             )
 
@@ -213,7 +215,7 @@
             old = top[q_block, rows_here]
             news = []
             for g in range(tile // group):
-                piece = scores[n][pl.ds(g * group, group)]
+                piece = score_refs[n][pl.ds(g * group, group)]
                 parts = [piece[:, m * HD : (m + 1) * HD] for m in range(chunks)]
                 if diagonal:
                     row = core * part + first_row + g * group
@@ -224,7 +226,7 @@
                 new = jnp.maximum(old[g * group : (g + 1) * group], jnp.max(most, axis=1, keepdims=True))
                 news.append(new)
                 weight = [jnp.exp2((one - new) * scale).astype(jnp.bfloat16) for one in parts]
-                shares[n][pl.ds(g * group, group)] = jnp.concatenate(weight, axis=1)
+                share_refs[n][pl.ds(g * group, group)] = jnp.concatenate(weight, axis=1)
             new = jnp.concatenate(news, axis=0)
             top[q_block, rows_here] = new
             return jnp.exp2((old - new) * scale)
@@ -234,7 +236,7 @@
             rows_here = pl.ds(first_row, tile)
             values = kv_in[k_block, 1]
             values = jnp.concatenate([values, jnp.ones_like(values)], axis=1)
-            product = jnp.dot(shares[n][...], values, preferred_element_type=jnp.float32)
+            product = jnp.dot(share_refs[n][...], values, preferred_element_type=jnp.float32)
             factor = jnp.concatenate([factor, factor], axis=1)
             accum[q_block, rows_here] = accum[q_block, rows_here] * factor + product
 
@@ -257,7 +259,10 @@
     mine = [half_rows(core, t) for t in range(2)]
     theirs = [half_rows(other, t) for t in range(2)]
     far_rows = [
-        [pl.ds(pl.multiple_of(core * part + t * tile + n * (tile // 2), 128), tile // 2) for n in range(2)]
+        [
+            pl.ds(pl.multiple_of(core * part + offsets[t] + n * (sizes[t] // 2), 64), sizes[t] // 2)
+            for n in range(2)
+        ]
         for t in range(2)
     ]
 
@@ -365,70 +370,77 @@
 
         ahead = BLOCKS - 2
 
-        def take(turn, carry):
-            t, step = turn // BLOCKS, lax.rem(turn, BLOCKS)
+        def take(step, carry):
             for late, away in zip(range(BLOCKS - 3, BLOCKS), (1, 3, 2)):
-                @pl.when(turn == late)
+                @pl.when(step == late)
                 def _():
                     hand_across(away)
 
-            @pl.when(turn < ahead)
+            @pl.when(step < ahead)
             def _():
-                receive(turn + 1)
-
-            @pl.when((turn > ahead) & (turn < BLOCKS))
+                receive(step + 1)
+
+            @pl.when(step > ahead)
             def _():
-                receive(turn)
-
-            block = jnp.where(t == 0, block_at(step), step)
-
-            @pl.when(t == 0)
-            def _():
-                pltpu.make_async_copy(q_in.at[block], q_in.at[block], q_sem.at[block]).wait()
-                q_two[block, :, pl.ds(0, HD)] = q_in[block]
-                shared(block).wait()
-                keys_across[block, pl.ds(0, HD)] = kv_in[block, 0].T
+                receive(step)
+
+            block = block_at(step)
+            pltpu.make_async_copy(q_in.at[block], q_in.at[block], q_sem.at[block]).wait()
+            q_two[block, :, pl.ds(0, HD)] = q_in[block]
+            shared(block).wait()
+            keys_across[block, pl.ds(0, HD)] = kv_in[block, 0].T
 
             def with_past(before):
-                past = jnp.where(t == 0, block_at(before), before)
+                past = block_at(before)
                 return jnp.maximum(block, past), jnp.minimum(block, past), False
 
+            def two_at_once(count, inner):
+                attend([with_past(2 * count + n) for n in range(2)], 0)
+                return inner
+
+            lax.fori_loop(0, step // 2, two_at_once, 0)
+            for rest in range(2):
+                @pl.when(lax.rem(step, 2) == rest)
+                def _():
+                    attend([with_past(step - 1 - n) for n in range(rest)] + [(block, block, True)], 0)
+
+            return carry
+
+        lax.fori_loop(0, BLOCKS, take, 0)
+
+        def finish_all(count, carry):
+            finish(block_at(BLOCKS - 1 - count), 0)
+            return carry
+
+        lax.fori_loop(0, BLOCKS, finish_all, 0)
+
+        def take_rest(block, carry):
             def four_at_once(count, inner):
-                attend([with_past(4 * count + n) for n in range(4)], t)
+                attend([(block, 4 * count + n, False) for n in range(4)], 1)
                 return inner
 
-            lax.fori_loop(0, step // 4, four_at_once, 0)
+            lax.fori_loop(0, block // 4, four_at_once, 0)
             for rest in range(4):
-                @pl.when(lax.rem(step, 4) == rest)
-                def _():
-                    attend([with_past(step - 1 - n) for n in range(rest)] + [(block, block, True)], t)
-
-            @pl.when(t == 1)
-            def _():
-                finish(block, 1)
-
-            @pl.when(turn == BLOCKS - 1)
-            def _():
-                def finish_all(count, inner):
-                    finish(block_at(BLOCKS - 1 - count), 0)
-                    return inner
-
-                lax.fori_loop(0, BLOCKS, finish_all, 0)
-
-            for when, action in ((BLOCKS + 5, send_own), (BLOCKS + 6, pass_on), (BLOCKS + 7, take_far)):
-                @pl.when(turn == when)
+                @pl.when(lax.rem(block, 4) == rest)
+                def _():
+                    attend([(block, block - 1 - n, False) for n in range(rest)] + [(block, block, True)], 1)
+
+            finish(block, 1)
+
+            for when, action in ((BLOCKS - 4, send_own), (BLOCKS - 2, pass_on)):
+                @pl.when(block == when)
                 def _():
                     each(action, 0)
 
             return carry
 
-        lax.fori_loop(0, 2 * BLOCKS, take, 0)
+        lax.fori_loop(0, BLOCKS, take_rest, 0)
 
     @pl.when(jnp.logical_not(works))
     def _():
         for away in (1, 3, 2):
             hand_across(away)
-        for action in (send_own, pass_on, take_far):
+        for action in (send_own, pass_on):
             each(action, 0)
 
     def half_landed(away, t):
@@ -439,7 +451,7 @@
     def project(aways, t, start, last):
         def some_rows(c, carry):
             span = half_rows(c, t)
-            product = None if start else total[pl.ds(pl.multiple_of(c * tile, 128), tile)]
+            product = None if start else total[pl.ds(pl.multiple_of(c * sizes[t], 128), sizes[t])]
             for away in aways:
                 source = lax.rem(z + away, RING)
                 term = jnp.dot(
@@ -450,12 +462,13 @@
             if last:
                 out_ref[span] = product.astype(jnp.bfloat16)
             else:
-                total[pl.ds(pl.multiple_of(c * tile, 128), tile)] = product
+                total[pl.ds(pl.multiple_of(c * sizes[t], 128), sizes[t])] = product
             return carry
 
         lax.fori_loop(0, 2, some_rows, 0)
 
     each(send_own, 1)
+    each(take_far, 0)
     for away in range(RING):
         half_landed(away, 0)
         weights_here(away)
@@ -506,6 +519,7 @@
     out_cols = w_out.shape[1] // lax.axis_size("head")
     dma = pltpu.SemaphoreType.DMA
     pairs = BLOCKS * (BLOCKS + 1) // 2
+    sizes = [part * 3 // 4] * 2 + [part // 4] * 4
     flops = pairs * part * rows * 4 * HD + 2 * rows * w_out.shape[1] * width
     return pl.pallas_call(
         kernel,
@@ -519,8 +533,8 @@
             pltpu.VMEM((BLOCKS, 2 * HD, rows), jnp.bfloat16),
             pltpu.VMEM((BLOCKS, part, HD), jnp.float32),
             pltpu.VMEM((BLOCKS, part, 2 * HD), jnp.float32),
-            [pltpu.VMEM((part // 2, rows), jnp.float32)] * 4,
-            [pltpu.VMEM((part // 2, rows), jnp.bfloat16)] * 4,
+            [pltpu.VMEM((size, rows), jnp.float32) for size in sizes],
+            [pltpu.VMEM((size, rows), jnp.bfloat16) for size in sizes],
             pltpu.VMEM((BLOCKS, part, HD), jnp.bfloat16),
             pltpu.VMEM((RING, rows, 2 * width), jnp.bfloat16),
             pltpu.VMEM((RING, 2, 2, width // 2, out_cols), jnp.bfloat16),

time: 110 us -> 113 us (1.027)
  Pallas kernels: 107 us -> 110 us
    pallas_call x1, Pallas kernels: 107 us -> 110 us  [per_device(): pl.pallas_call(kernel, out_shape=jax.ShapeDtypeStruct((rows, out_cols), j...]
where the time goes in v5:
time: 113 us
  Pallas kernels  110 us (97%)
  local copies, waits for them, and re-layouts  2.49 us (2%)
    pallas_call x1, Pallas kernels, per_device(): pl.pallas_call(kernel, out_shape=jax.ShapeDtypeStruct((rows, out_cols), j...  110 us
    unnamed x1, local copies, waits for them, and re-layouts  2.49 us

profile of v5, /device:TPU:1, one launch (start us, length us, event | category | flops | bytes accessed | tf_op | source)
XLA Modules:
  0.0 112.8 jit_solution(2249638097462779609)
XLA Ops:
  0.0 110.4 %shard_map.55 = bf16[1024,640]{1,0:T(8,128)(2,1)} custom-call(s32[8]{0:T(128)} %lengths_ref.1, bf16[1024,384]{1,0:T(8,128)(2,1)} %q_ref.1, bf16[1024,384]{1,0:T(8,128)(2,1)} %k_ref.1, bf16[1024,384]{1,0:T(8,128)(2,1)} %v_ref.1, bf16[2,192,5120]{2,1,0:T(8,128)(2,1)} %bitcast.1), custom_call_target="tpu_custom_call" | custom-call | flops 13690208256 | bytes 16777216 | tf_op jit(solution)/shard_map/pallas_call | solution.py:524
  110.4 2.5 %copy.7 = bf16[1024,640]{1,0:T(8,128)(2,1)} copy(bf16[1024,640]{1,0:T(8,128)(2,1)} %shard_map.55) | data formatting | bytes 2621440

commit v6 on v4

--- a/solution.py
+++ b/solution.py
@@ -198,14 +198,14 @@
         def _():
             mixed_copy(block, t).start()
 
-    def attend(tiles, t):
+    def score(slot, q_block, k_block, t):
+        scores[slot][...] = jnp.dot(
+            q_two[q_block, pl.ds(pl.multiple_of(t * tile, 128), tile)], keys_across[k_block],
+            preferred_element_type=jnp.float32,
+        )
+
+    def attend(tiles, t, following):
         first_row = pl.multiple_of(t * tile, 128)
-
-        def score(n):
-            q_block, k_block, _ = tiles[n]
-            scores[n][...] = jnp.dot(
-                q_two[q_block, pl.ds(first_row, tile)], keys_across[k_block], preferred_element_type=jnp.float32
-            )
 
         def soften(n):
             q_block, _, diagonal = tiles[n]
@@ -238,11 +238,15 @@
             factor = jnp.concatenate([factor, factor], axis=1)
             accum[q_block, rows_here] = accum[q_block, rows_here] * factor + product
 
-        score(0)
         for n in range(len(tiles)):
             if n + 1 < len(tiles):
-                score(n + 1)
-            mix(n, soften(n))
+                score(n + 1, *tiles[n + 1][:2], t)
+            elif n > 0:
+                score(0, *following)
+            factor = soften(n)
+            if len(tiles) == 1:
+                score(0, *following)
+            mix(n, factor)
 
     order = [(dx, dy) for dy in (2, 1, 3, 0) for dx in (1, 0)]
 
@@ -393,15 +397,32 @@
                 past = jnp.where(t == 0, block_at(before), before)
                 return jnp.maximum(block, past), jnp.minimum(block, past), False
 
+            whole = lax.rem(step, 4) == 0
+            rest_q, rest_k, _ = with_past(jnp.maximum(step - 1, 0))
+            rest_q, rest_k = jnp.where(whole, block, rest_q), jnp.where(whole, block, rest_k)
+            turning = turn == BLOCKS - 1
+            next_q = jnp.where(turning, 0, jnp.where(t == 1, jnp.minimum(step + 1, BLOCKS - 1), block))
+            next_k = jnp.where(turning | ((t == 1) & (step >= 3)), 0, jnp.where(t == 1, step, block))
+            next_t = jnp.where(turning, 1, t)
+
+            @pl.when((t == 0) & (step < 4))
+            def _():
+                score(0, rest_q, rest_k, t)
+
+            @pl.when((t == 0) & (step >= 4))
+            def _():
+                score(0, *with_past(0)[:2], t)
+
             def four_at_once(count, inner):
-                attend([with_past(4 * count + n) for n in range(4)], t)
+                attend([with_past(4 * count + n) for n in range(4)], t, (rest_q, rest_k, t))
                 return inner
 
             lax.fori_loop(0, step // 4, four_at_once, 0)
             for rest in range(4):
                 @pl.when(lax.rem(step, 4) == rest)
                 def _():
-                    attend([with_past(step - 1 - n) for n in range(rest)] + [(block, block, True)], t)
+                    pairs = [with_past(step - 1 - n) for n in range(rest)] + [(block, block, True)]
+                    attend(pairs, t, (next_q, next_k, next_t))
 
             @pl.when(t == 1)
             def _():

time: 110 us -> 110 us (level)
  no operation moved by 1% of the time
where the time goes in v6:
time: 110 us
  Pallas kernels  107 us (97%)
  local copies, waits for them, and re-layouts  2.49 us (2%)
    pallas_call x1, Pallas kernels, per_device(): pl.pallas_call(kernel, out_shape=jax.ShapeDtypeStruct((rows, out_cols), j...  107 us
    unnamed x1, local copies, waits for them, and re-layouts  2.49 us

profile of v6, /device:TPU:1, one launch (start us, length us, event | category | flops | bytes accessed | tf_op | source)
XLA Modules:
  0.0 109.7 jit_solution(13035415542397349970)
XLA Ops:
  0.0 107.2 %shard_map.55 = bf16[1024,640]{1,0:T(8,128)(2,1)} custom-call(s32[8]{0:T(128)} %lengths_ref.1, bf16[1024,384]{1,0:T(8,128)(2,1)} %q_ref.1, bf16[1024,384]{1,0:T(8,128)(2,1)} %k_ref.1, bf16[1024,384]{1,0:T(8,128)(2,1)} %v_ref.1, bf16[2,192,5120]{2,1,0:T(8,128)(2,1)} %bitcast.1), custom_call_target="tpu_custom_call" | custom-call | flops 13690208256 | bytes 16777216 | tf_op jit(solution)/shard_map/pallas_call | solution.py:531
  107.2 2.5 %copy.7 = bf16[1024,640]{1,0:T(8,128)(2,1)} copy(bf16[1024,640]{1,0:T(8,128)(2,1)} %shard_map.55) | data formatting | bytes 2621440

commit v7 on v4

--- a/solution.py
+++ b/solution.py
@@ -18,8 +18,8 @@
 
 def kernel(
     lengths_ref, q_ref, k_ref, v_ref, w_ref, out_ref,
-    q_in, kv_in, q_two, keys_across, top, accum, scores, shares, mixed, gathered, weights, total,
-    send_sem, q_sem, kv_sem, share_send, share_sem, mixed_send, mixed_sem,
+    laid, q_in, kv_in, q_two, keys_across, top, accum, scores, shares, mixed, gathered, weights, total,
+    laid_sem, send_sem, q_sem, kv_sem, share_send, share_sem, mixed_send, mixed_sem,
     w_send, w_sem, across_send, across_sem, ring_send, ring_sem, relay_send, relay_sem, pair_send, pair_sem,
 ):
     rows = q_ref.shape[0]
@@ -38,6 +38,14 @@
     works = place_y < heads
     partner = ((RING - 1 - ctx // RING) * RING + place_y, head)
 
+    def lay_out(n, local):
+        source = (k_ref, v_ref, q_ref)[n].at[:, pl.ds(local * HD, HD)]
+        return pltpu.make_async_copy(source, laid.at[n, local], laid_sem.at[n, local])
+
+    for n in range(3):
+        for local in range(heads):
+            lay_out(n, local).start()
+
     barrier = pltpu.get_barrier_semaphore()
     for block in range(BLOCKS):
         for c in range(2):
@@ -57,18 +65,18 @@
     def outgoing(away, c, n):
         local = lax.rem(place_y + away, RING)
         target = core * RING + local
-        cols = pl.ds(pl.multiple_of(local * HD, HD), HD)
         span = pl.ds(c * part, part)
-        source, dest, sem = (
-            (k_ref, kv_in.at[place, 0, span], kv_sem.at[place]),
-            (v_ref, kv_in.at[place, 1, span], kv_sem.at[place]),
-            (q_ref, q_in.at[place], q_sem.at[place]),
+        source = laid.at[n, jnp.minimum(local, heads - 1), span]
+        dest, sem = (
+            (kv_in.at[place, 0, span], kv_sem.at[place]),
+            (kv_in.at[place, 1, span], kv_sem.at[place]),
+            (q_in.at[place], q_sem.at[place]),
         )[n]
         here = target == place
 
         def remote():
             return pltpu.make_async_remote_copy(
-                src_ref=source.at[span, cols], dst_ref=dest, send_sem=send_sem.at[away, c, n], recv_sem=sem,
+                src_ref=source, dst_ref=dest, send_sem=send_sem.at[away, c, n], recv_sem=sem,
                 device_id=(first + target, z * 2 + c), device_id_type=MESH,
             )
 
@@ -76,7 +84,7 @@
             if away == 0:
                 @pl.when((local < heads) & here & (core == c))
                 def _():
-                    pltpu.make_async_copy(source.at[span, cols], dest, sem).start()
+                    pltpu.make_async_copy(source, dest, sem).start()
 
                 @pl.when((local < heads) & jnp.logical_not(here & (core == c)))
                 def _():
@@ -140,7 +148,9 @@
             pltpu.make_async_copy(piece, piece, across_sem.at[away]).wait()
 
     sends = [[outgoing(away, c, n) for away in (1, 3, 2, 0) for c in range(2)] for n in range(3)]
-    for group, away in zip(sends, (2, 1, 3)):
+    for n, (group, away) in enumerate(zip(sends, (2, 1, 3))):
+        for local in range(heads):
+            lay_out(n, local).wait()
         for start, _ in group:
             start()
         for c in range(2):
@@ -367,7 +377,7 @@
 
         def take(turn, carry):
             t, step = turn // BLOCKS, lax.rem(turn, BLOCKS)
-            for late, away in zip(range(BLOCKS - 3, BLOCKS), (1, 3, 2)):
+            for late, away in ((BLOCKS - 1, 1), (BLOCKS - 1, 3), (BLOCKS - 1, 2)):
                 @pl.when(turn == late)
                 def _():
                     hand_across(away)
@@ -513,6 +523,7 @@
         in_specs=[pl.BlockSpec(memory_space=pltpu.SMEM)] + [pl.BlockSpec(memory_space=pl.ANY)] * 4,
         out_specs=pl.BlockSpec(memory_space=pltpu.VMEM),
         scratch_shapes=[
+            pltpu.VMEM((3, heads, rows, HD), jnp.bfloat16),
             pltpu.VMEM((BLOCKS, part, HD), jnp.bfloat16),
             pltpu.VMEM((BLOCKS, 2, rows, HD), jnp.bfloat16),
             pltpu.VMEM((BLOCKS, part, 2 * HD), jnp.bfloat16),
@@ -525,6 +536,7 @@
             pltpu.VMEM((RING, rows, 2 * width), jnp.bfloat16),
             pltpu.VMEM((RING, 2, 2, width // 2, out_cols), jnp.bfloat16),
             pltpu.VMEM((part, out_cols), jnp.float32),
+            dma((3, heads)),
             dma((RING, 2, 3)),
             dma((BLOCKS,)),
             dma((BLOCKS,)),

time: 110 us -> 110 us (level)
  no operation moved by 1% of the time
where the time goes in v7:
time: 110 us; the launch traced here: 109 us
  Pallas kernels  106 us (96%)
  local copies, waits for them, and re-layouts  2.49 us (2%)
    pallas_call x1, Pallas kernels, per_device(): pl.pallas_call(kernel, out_shape=jax.ShapeDtypeStruct((rows, out_cols), j...  106 us
    unnamed x1, local copies, waits for them, and re-layouts  2.49 us

profile of v7, /device:TPU:1, one launch (start us, length us, event | category | flops | bytes accessed | tf_op | source)
XLA Modules:
  0.0 109.0 jit_solution(8438038912128878339)
XLA Ops:
  0.0 106.5 %shard_map.55 = bf16[1024,640]{1,0:T(8,128)(2,1)} custom-call(s32[8]{0:T(128)} %lengths_ref.1, bf16[1024,384]{1,0:T(8,128)(2,1)} %q_ref.1, bf16[1024,384]{1,0:T(8,128)(2,1)} %k_ref.1, bf16[1024,384]{1,0:T(8,128)(2,1)} %v_ref.1, bf16[2,192,5120]{2,1,0:T(8,128)(2,1)} %bitcast.1), custom_call_target="tpu_custom_call" | custom-call | flops 13690208256 | bytes 16777216 | tf_op jit(solution)/shard_map/pallas_call | solution.py:520
  106.5 2.5 %copy.7 = bf16[1024,640]{1,0:T(8,128)(2,1)} copy(bf16[1024,640]{1,0:T(8,128)(2,1)} %shard_map.55) | data formatting | bytes 2621440
